TPU v7x, 256 devices: a whole 4x4x8 slice. The times are simulated.
256 devices in a mesh: dp: 8 (over y, core), seq: 32 (over x, z).
Axes of the slice: x: 4, y: 4, z: 8, core: 2. Of those that a mesh axis runs over, the one named last changes fastest.
Arguments:
- inputs: bfloat16 [8, 4096, 4096], P('dp', 'seq'), may hold values from -6 to 6
- gates: bfloat16 [8, 4096, 4096], P('dp', 'seq'), may hold values from -6 to 6
- keys_b: bfloat16 [8, 4096, 128], P('dp', 'seq'), may hold values from -2 to 2
- reads_c: bfloat16 [8, 4096, 128], P('dp', 'seq'), may hold values from -2 to 2
- step_codes: int32 [8, 4096], P('dp', 'seq'), may hold values from 1 to 16
- seg_starts: int32 [8, 4096], P('dp', 'seq'), may hold values 0 or 1
- targets: bfloat16 [8, 4096, 4096], P('dp', 'seq'), may hold values from -6 to 6
- log_rates: float32 [64], replicated
- skips: float32 [64], replicated, may hold values from 0.5 to 2
- gains: float32 [4096], replicated, may hold values from 0.5 to 1.5
Outputs:
- loss: float32 [], replicated
- grad_inputs: bfloat16 [8, 4096, 4096], P('dp', 'seq')
- grad_gates: bfloat16 [8, 4096, 4096], P('dp', 'seq')
- grad_keys: bfloat16 [8, 4096, 128], P('dp', 'seq')
- grad_reads: bfloat16 [8, 4096, 128], P('dp', 'seq')
- grad_rates: float32 [64], replicated
- grad_skips: float32 [64], replicated
- grad_gains: float32 [4096], replicated
All inputs are finite; a program needn't handle non-finite values. No bound on the sum of `seg_starts` on one device may be relied on, other than what follows from the above.
Results may differ from a plain program's by a relative error of at most 0.012.
Values sent between devices are 32-bit elements; how exact they have to be, the bound alone decides.
A program may use at most 192 MiB of HBM per device.

v0:
```python
import jax
import jax.numpy as jnp
from jax import lax
from jax.sharding import PartitionSpec as P


def prefix(shard, axis, combine, identity, reverse):
    count, index = (lax.axis_size(axis), lax.axis_index(axis))
    everything = jax.tree.map(lambda part: lax.all_gather(part, axis), shard)
    start = jax.tree.map(
        lambda part, zero: jnp.broadcast_to(jnp.asarray(zero, part.dtype), part.shape),
        shard,
        identity,
    )

    def hop(k, before):
        at = count - 1 - k if reverse else k
        reached = at > index if reverse else at < index
        new = combine(before, jax.tree.map(lambda part: part[at], everything))
        return jax.tree.map(lambda a, b: jnp.where(reached, a, b), new, before)

    return lax.fori_loop(0, count, hop, start)


def decays(step_codes, seg_starts, log_rates):
    timestep = step_codes.astype(jnp.float32) / 64.0
    rate_vals = jnp.exp(log_rates)
    cumulative = jnp.cumsum(-timestep[:, None] * rate_vals[None, :], axis=0)
    segment = jnp.cumsum(seg_starts, axis=0, dtype=jnp.int32)
    return (timestep, cumulative, segment)


def local_state(inputs, keys_b, step_codes, seg_starts, log_rates):
    timestep, cumulative, segment = decays(step_codes, seg_starts, log_rates)
    n_heads = log_rates.shape[0]
    inner_width = inputs.shape[1]
    head_size = inner_width // n_heads
    keep_end = (segment == segment[-1]).astype(jnp.float32)
    weight = jnp.exp(cumulative[-1][None, :] - cumulative) * keep_end[:, None] * timestep[:, None]
    wide_weight = jnp.repeat(weight, head_size, axis=1)
    scaled = (inputs.astype(jnp.float32) * wide_weight).astype(jnp.bfloat16)
    state_flat = lax.dot_general(
        scaled, keys_b, (((0,), (0,)), ((), ())), preferred_element_type=jnp.float32
    )
    state_sum = state_flat.reshape(n_heads, head_size, keys_b.shape[1])
    unbroken = (segment[-1] == 0).astype(jnp.float32)
    growth = unbroken * jnp.exp(cumulative[-1])
    return (state_sum, growth)


def intra_block(inner_cb, visible, timestep, cumulative, x_cols):
    spread_log = cumulative.T[:, :, None] - cumulative.T[:, None, :]
    decay_tab = jnp.where(visible[None], jnp.exp(jnp.where(visible[None], spread_log, 0.0)), 0.0)
    scores = (inner_cb[None] * decay_tab * timestep[None, None, :]).astype(jnp.bfloat16)
    return lax.dot_general(
        x_cols, scores, (((2,), (2,)), ((0,), (0,))), preferred_element_type=jnp.float32
    )


def local_output(
    inputs,
    gates,
    keys_b,
    reads_c,
    step_codes,
    seg_starts,
    targets,
    log_rates,
    skips,
    gains,
    incoming,
):
    timestep, cumulative, segment = decays(step_codes, seg_starts, log_rates)
    length = inputs.shape[0]
    n_heads = log_rates.shape[0]
    inner_width = inputs.shape[1]
    head_size = inner_width // n_heads
    carried = (segment == 0).astype(jnp.float32)[:, None] * jnp.exp(cumulative)
    inner_cb = jnp.dot(reads_c, keys_b.T, preferred_element_type=jnp.float32)
    positions = jnp.arange(length)
    visible = (positions[:, None] >= positions[None, :]) & (segment[:, None] == segment[None, :])
    x_cols = inputs.T.reshape(n_heads, head_size, length)
    inside = intra_block(inner_cb, visible, timestep, cumulative, x_cols)
    entering_flat = jnp.dot(
        incoming.reshape(inner_width, -1),
        reads_c.astype(jnp.float32).T,
        precision=lax.Precision.HIGHEST,
    )
    entering = carried.T[:, None, :] * entering_flat.reshape(n_heads, head_size, length)
    mixture = inside + entering + skips[:, None, None] * x_cols.astype(jnp.float32)
    gated_vals = mixture.reshape(inner_width, length) * jax.nn.silu(gates.T.astype(jnp.float32))
    normed = (
        gated_vals
        * lax.rsqrt(jnp.mean(gated_vals * gated_vals, axis=0, keepdims=True) + 1e-05)
        * gains[:, None]
    )
    mismatch = normed - targets.T.astype(jnp.float32)
    return 0.5 * jnp.sum(mismatch * mismatch)


def combine_pair(earlier, later):
    return (earlier[0] * later[0], later[0][:, :, None, None] * earlier[1] + later[1])


def shards(
    inputs, gates, keys_b, reads_c, step_codes, seg_starts, targets, log_rates, skips, gains
):

    def states_of(x_all, b_all, rate_logs):
        return jax.vmap(local_state, in_axes=(0, 0, 0, 0, None))(
            x_all, b_all, step_codes, seg_starts, rate_logs
        )

    (block_state, growth), state_pull = jax.vjp(states_of, inputs, keys_b, log_rates)
    incoming = prefix(
        (growth, block_state),
        "seq",
        combine_pair,
        (jnp.ones_like(growth), jnp.zeros_like(block_state)),
        False,
    )[1]

    def summed_loss(x_all, z_all, b_all, c_all, rate_logs, skip_vals, gain_vals, entering):
        losses = jax.vmap(local_output, in_axes=(0, 0, 0, 0, 0, 0, 0, None, None, None, 0))(
            x_all,
            z_all,
            b_all,
            c_all,
            step_codes,
            seg_starts,
            targets,
            rate_logs,
            skip_vals,
            gain_vals,
            entering,
        )
        return jnp.sum(losses)

    loss_here, pullback = jax.vjp(
        summed_loss, inputs, gates, keys_b, reads_c, log_rates, skips, gains, incoming
    )
    grad_x, grad_z, grad_b, grad_c, grad_rate, grad_skip, grad_gain, direct = pullback(
        jnp.float32(1.0)
    )
    beyond = prefix(
        (growth, direct), "seq", combine_pair, (jnp.ones_like(growth), jnp.zeros_like(direct)), True
    )[1]
    decay_grad = jnp.sum(beyond * incoming, axis=(2, 3))
    state_gx, state_gb, state_ga = state_pull((beyond, decay_grad))
    grad_x = (grad_x.astype(jnp.float32) + state_gx.astype(jnp.float32)).astype(jnp.bfloat16)
    grad_b = (grad_b.astype(jnp.float32) + state_gb.astype(jnp.float32)).astype(jnp.bfloat16)
    grad_rate = grad_rate + state_ga
    totals = lax.psum((loss_here, grad_rate, grad_skip, grad_gain), ("dp", "seq"))
    row_count = jnp.float32(
        inputs.shape[0] * lax.axis_size("dp") * inputs.shape[1] * lax.axis_size("seq")
    )
    return (
        totals[0] / row_count,
        grad_x,
        grad_z,
        grad_b,
        grad_c,
        totals[1] / row_count,
        totals[2] / row_count,
        totals[3] / row_count,
    )


def solution(mesh):
    placed = (
        P("dp", "seq", None),
        P("dp", "seq", None),
        P("dp", "seq", None),
        P("dp", "seq", None),
        P("dp", "seq"),
        P("dp", "seq"),
        P("dp", "seq", None),
        P(),
        P(),
        P(),
    )
    return jax.shard_map(
        shards,
        mesh=mesh,
        in_specs=placed,
        out_specs=(
            P(),
            P("dp", "seq", None),
            P("dp", "seq", None),
            P("dp", "seq", None),
            P("dp", "seq", None),
            P(),
            P(),
            P(),
        ),
        check_vma=False,
    )
```

profile of v0, /device:TPU:1, one launch (start us, length us, event | category | flops | bytes accessed | tf_op | source)
XLA Modules:
  0.0 1147.9 jit_solution(299511797859118505)
XLA Ops:
  17.3 2.3 copy.88
  19.6 2.3 copy.89
  21.9 37.4 %all_gather.12 = f32[32,1,64]{2,1,0:T(1,128)S(1)} all-gather(f32[1,1,64]{2,1,0:T(1,128)S(1)} %get-tuple-element.402), channel_id=1, replica_groups=mesh['dp'=8,'seq'=32] {'seq'}, dimensions={0}, use_global_device_ids=true | all-gather | bytes 8448 | tf_op jit(solution)/shard_map/all_gather | solution.py:9
  59.5 392.6 %all-gather.5.cloned.1.call-done = f32[2048,64,128]{2,1,0:T(8,128)} async-done(((f32[64,64,128]{2,1,0:T(8,128)}), f32[2048,64,128]{2,1,0:T(8,128)}) %all-gather.5.cloned.1.call-update) | async-done | bytes 67108880 | tf_op jit(solution)/shard_map/all_gather | solution.py:9
  452.1 68.1 %while.30 = (s32[]{:T(128)}, f32[1,64,64,128]{3,2,1,0:T(8,128)S(1)}, s32[]{:T(128)}, f32[32,1,64]{2,1,0:T(1,128)S(1)}, f32[32,1,64,64,128]{4,3,2,1,0:T(8,128)}, /*index=5*/s32[]{:T(128)}, s32[]{:T(128)}) while((s32[]{:T(128)}, f32[1,64,64,128]{3,2,1,0:T(8,128)S(1)}, s32[]{:T(128)}, f32[32,1,64]{2,1,0:T(1,128)S(1)}, ...), condition=%wide.region_3.4_spmd.clone, body=%wide.region_2.3_spmd.clone.sunk | while | flops 2097156 | bytes 6292337 | solution.py:22
  454.2 2.1 fusion.78
  456.4 2.1 fusion.78
  458.5 2.1 fusion.78
  460.6 2.1 fusion.78
  462.8 2.1 fusion.78
  464.9 2.1 fusion.78
  524.8 2.6 multiply_reduce_fusion.1
  527.4 3.5 multiply_reduce_fusion.2
  533.6 2.4 fusion.43
  536.8 2.9 multiply_reduce_fusion.4
  539.8 3.9 fusion.7
  545.0 2.4 copy.95
  548.1 6.3 fusion.25
  555.2 3.1 fusion.24
  558.3 406.3 %all-gather.7.cloned.1.call-done = f32[2048,64,128]{2,1,0:T(8,128)} async-done(((f32[64,64,128]{2,1,0:T(8,128)}), f32[2048,64,128]{2,1,0:T(8,128)}) %all-gather.7.cloned.1.call-update) | async-done | bytes 67108880 | tf_op jit(solution)/shard_map/all_gather | solution.py:9
  964.6 88.6 %while.31 = (s32[]{:T(128)}, f32[1,64,64,128]{3,2,1,0:T(8,128)S(1)}, s32[]{:T(128)}, f32[32,1,64]{2,1,0:T(1,128)}, f32[32,1,64,64,128]{4,3,2,1,0:T(8,128)}, /*index=5*/s32[]{:T(128)}, s32[]{:T(128)}, s32[]{:T(128)}, s32[]{:T(128)}) while((s32[]{:T(128)}, f32[1,64,64,128]{3,2,1,0:T(8,128)S(1)}, s32[]{:T(128)}, ...), condition=%wide.region_9.10_spmd.clone, body=%wide.region_8.9_spmd.clone.sunk | while | flops 2097160 | bytes 6292399 | solution.py:22
  1053.3 2.2 multiply_reduce_fusion.3
  1058.8 2.3 copy.94
  1062.9 75.3 %all-reduce.2 = (f32[]{:T(128)}, f32[64]{0:T(128)S(1)}, f32[64]{0:T(128)S(1)}, f32[4096]{0:T(1024)S(1)}) all-reduce(f32[]{:T(128)S(6)} %mul.510, f32[64]{0:T(128)S(1)} %add_multiply_fusion, f32[64]{0:T(128)S(1)} %copy-done.33, f32[4096]{0:T(1024)S(1)} %get-tuple-element.362), channel_id=1, replica_groups=mesh['dp'=8,'seq'=32] {'dp','seq'}, use_global_device_ids=true, to_apply=%region_6.7 | all-reduce | flops 4225 | bytes 33800 | tf_op jit(solution)/shard_map/psum | solution.py:153
  (248 shorter events, 167.6 us)
Async XLA Ops:
  7.2 8.2 copy-start
  7.2 444.9 %all-gather.5.cloned.1.call-start = ((), (), s32[]{:S(2)}) async-start(), calls=%async_computation | async-start | bytes 69206016 | tf_op jit(solution)/shard_map/all_gather | solution.py:9
  7.9 513.7 %copy-start.25 = (f32[128]{0:T(128)}, f32[128]{0:T(128)S(1)}, u32[]{:S(2)}) copy-start(f32[128]{0:T(128)S(1)} %multiply_bitcast_fusion.1) | copy-start | bytes 1540
  8.6 3.9 copy-start.31
  12.1 47.3 %copy-start.29 = (f32[128]{0:T(128)}, f32[128]{0:T(128)S(1)}, u32[]{:S(2)}) copy-start(f32[128]{0:T(128)S(1)} %get-tuple-element.403) | copy-start | bytes 1540
  17.2 947.5 %all-gather.7.cloned.1.call-start = ((), (), s32[]{:S(2)}) async-start(), calls=%async_computation.1 | async-start | bytes 69206016 | tf_op jit(solution)/shard_map/all_gather | solution.py:9
  17.3 42.0 %copy-start.13 = (f32[4096]{0:T(1024)S(1)}, f32[4096]{0:T(1024)}, u32[]{:S(2)}) copy-start(f32[4096]{0:T(1024)} %param.23) | copy-start | bytes 49156
  17.3 42.1 %copy-start.12 = (bf16[1,128,128]{2,1,0:T(8,128)(2,1)S(1)}, bf16[1,128,128]{2,1,0:T(8,128)(2,1)}, u32[]{:S(2)}) copy-start(bf16[1,128,128]{2,1,0:T(8,128)(2,1)} %param.17) | copy-start | bytes 98308
  59.3 462.2 %copy-start.18 = (pred[128,128]{1,0:T(8,128)(4,1)}, pred[128,128]{1,0:T(8,128)(4,1)S(1)}, u32[]{:S(2)}) copy-start(pred[128,128]{1,0:T(8,128)(4,1)S(1)} %fusion.42) | copy-start | bytes 49156
  59.5 462.0 %copy-start.14 = (f32[128,128]{1,0:T(8,128)}, f32[128,128]{1,0:T(8,128)S(1)}, u32[]{:S(2)}) copy-start(f32[128,128]{1,0:T(8,128)S(1)} %fusion.52) | copy-start | bytes 196612
  536.8 3.0 copy-start.4
  536.8 3.0 copy-start.15
  536.8 3.0 copy-start.19
  536.8 3.0 copy-start.26
  539.8 3.9 copy-start.30
  548.0 7.1 copy-start.5
  548.0 7.1 copy-start.16
  548.0 7.1 copy-start.20
  548.1 7.1 copy-start.27
  548.1 7.1 copy-start.36
  1058.7 2.7 copy-start.28
  1058.7 4.0 copy-start.32
  1058.7 4.1 copy-start.34
  1058.8 4.1 copy-start.33
  (15 other events, 25.9 us)
Sparse Core Ops, SparseCore 0:
  17.3 434.7 all-gather.4
  536.1 428.4 all-gather.6
where the time goes:
time: 1150 us
  waiting for transfers between devices  799 us (69%)
  other arithmetic  155 us (13%)
  blocking collectives  113 us (10%)
  local copies, waits for them, and re-layouts  38.3 us (3%)
  matrix products  23.1 us (2%)
  between operations  17.7 us (2%)
    all_gather x2, waiting for transfers between devices, prefix(): everything = jax.tree.map(lambda part: lax.all_gather(part, axis), shard)  799 us
    select_n x64, other arithmetic, hop(): return jax.tree.map(lambda a, b: jnp.where(reached, a, b), new, before)  133 us
    psum x1, blocking collectives, shards(): lax.psum((loss_here, grad_rate, grad_skip, grad_gain), ('dp', 'seq'))  75.3 us
    all_gather x1, blocking collectives, prefix(): everything = jax.tree.map(lambda part: lax.all_gather(part, axis), shard)  37.4 us
  transfers between devices with their start and end apart: 2, of which 2 were waited for; matrix products, arithmetic and copies ran while one was open for 2% of the time, Pallas kernels for 0%

commit v1 on v0

v1 whole, which is shorter than its diff:
```python
import functools

import jax
import jax.numpy as jnp
from jax import lax
from jax.experimental import pallas as pl
from jax.experimental.pallas import tpu as pltpu
from jax.sharding import PartitionSpec as P

F32, BF16 = jnp.float32, jnp.bfloat16
LANES = 128
Z_RING = 8
SPLIT = 2
LAG = (9, 8)


def red8(v):
    return v.reshape(v.shape[0] // 8, 8, LANES).sum(axis=0)


def mm(a, b):
    return lax.dot_general(a, b, (((1,), (0,)), ((), ())), preferred_element_type=F32)


def mm_nt(a, b):
    return lax.dot_general(a, b, (((1,), (1,)), ((), ())), preferred_element_type=F32)


def mm_tn(a, b):
    return lax.dot_general(a, b, (((0,), (0,)), ((), ())), preferred_element_type=F32)


def kernel(
    xr, zr, dpn, nb, rows_total,
    lr, sk, x, z, tg, bk, ck, codes, segs, gains,
    gx, gz, gb, gc, red,
    s_st, p_st, k_st, d_st, r_st, q_st,
    mix, ebuf, dxa, inter, ub,
    cols, tab, acc, ga, sa, ra, bt, ct, meta, arz, arx, ard,
    f_recv, f_carry, b_recv, b_carry, sends, msems,
    z_ss, z_rs, x_ss, x_rs, d_ss, d_rs,
):
    tok = x.shape[0]
    width = nb * LANES
    me, dpi = lax.axis_index("seq"), lax.axis_index("dp")
    zi, xi = lax.rem(me, zr), lax.div(me, zr)
    z_at = lambda k: {"seq": xi * zr + lax.rem(zi + k, zr)}
    x_at = lambda k: {"seq": lax.rem(xi + k, xr) * zr + zi}
    d_at = lambda k: {"dp": lax.rem(dpi + k, dpn)}

    barrier = pltpu.get_barrier_semaphore()
    peers = [z_at(k) for k in range(1, zr)] + [x_at(k) for k in range(1, xr)] + [d_at(k) for k in range(1, dpn)]
    for peer in peers:
        pl.semaphore_signal(barrier, inc=1, device_id=peer, device_id_type=pl.DeviceIdType.MESH)

    t_i = lax.broadcasted_iota(jnp.int32, (tok, tok), 0)
    s_i = lax.broadcasted_iota(jnp.int32, (tok, tok), 1)
    diag, upto = t_i == s_i, s_i <= t_i

    def forms(row):
        wide = jnp.broadcast_to(row, (tok, tok))
        own = jnp.sum(jnp.where(diag, wide, 0.0), axis=1, keepdims=True)
        col = jnp.sum(jnp.where(upto, wide, 0.0), axis=1, keepdims=True)
        across = jnp.sum(jnp.where(t_i <= s_i, jnp.broadcast_to(own, (tok, tok)), 0.0), axis=0, keepdims=True)
        return own, col, across, jnp.sum(row, axis=1, keepdims=True)

    code_row = codes[...].astype(F32)
    code_own, cum_col, cum_row, cum_end = forms(code_row)
    _, seg_col, seg_row, seg_end = forms(segs[...].astype(F32))
    visible = upto & (seg_col == seg_row)
    c_mat, b_mat = ck[...], bk[...]
    dt_row = code_row * (1.0 / 64.0)
    gap = jnp.where(visible, (cum_col - cum_row) * (1.0 / 64.0), 0.0)
    dt_vis = jnp.where(visible, jnp.broadcast_to(dt_row, (tok, tok)), 0.0)
    cb_dt = mm_nt(c_mat, b_mat) * dt_vis
    tab[0], tab[1], tab[2], tab[3] = gap, cb_dt, cb_dt * gap, dt_vis
    shape = (tok, LANES)
    cols[0] = jnp.broadcast_to(cum_col * (1.0 / 64.0), shape)
    cols[1] = jnp.broadcast_to((cum_end - cum_col) * (1.0 / 64.0), shape)
    cols[2] = jnp.broadcast_to(jnp.where(seg_col == seg_end, code_own * (1.0 / 64.0), 0.0), shape)
    cols[3] = jnp.broadcast_to((seg_col == 0.0).astype(F32), shape)
    bt[...], ct[...] = b_mat.astype(F32).T.astype(BF16), c_mat.astype(F32).T.astype(BF16)
    end_dt = jnp.broadcast_to(cum_end * (1.0 / 64.0), (1, LANES))
    broken = jnp.broadcast_to((seg_end > 0.0).astype(F32), (1, LANES))
    meta[6] = jnp.where(
        lax.broadcasted_iota(jnp.int32, (8, LANES), 0) == 0, end_dt,
        jnp.where(lax.broadcasted_iota(jnp.int32, (8, LANES), 0) == 1, broken, 0.0),
    )
    acc[...] = jnp.zeros_like(acc)

    low = lax.broadcasted_iota(jnp.int32, (1, LANES), 1) < LANES // 2

    def rates(b):
        a0 = jnp.exp(jnp.full((1, LANES), lr[2 * b], F32))
        a1 = jnp.exp(jnp.full((1, LANES), lr[2 * b + 1], F32))
        return a0, a1, jnp.where(low, a0, a1)

    def skip_row(b):
        return jnp.where(low, jnp.full((1, LANES), sk[2 * b], F32), jnp.full((1, LANES), sk[2 * b + 1], F32))

    def decay_of(m, a):
        return jnp.where(m[1:2] > 0.0, 0.0, jnp.exp(-a * m[0:1]))

    def lanes(b):
        return pl.ds(pl.multiple_of(b * LANES, LANES), LANES)

    def pair(b):
        xb = x[:, lanes(b)]
        zero = jnp.zeros_like(xb)
        return jnp.concatenate([jnp.where(low, xb, zero), jnp.where(low, zero, xb)], axis=0)

    part = tok // SPLIT

    class Pass:
        def __init__(self, pos, row, up, down, across, out, recv, carry, recv_sem, carry_sem, sem0):
            self.pos, self.row, self.up, self.down, self.across = pos, row, up, down, across
            self.out, self.recv, self.carry = out, recv, carry
            self.recv_sem, self.carry_sem, self.sem0 = recv_sem, carry_sem, sem0
            self.lag = jnp.where(row == 0, 0, lax.div((2 * (zr - 1) + row - 2 * pos) * LAG[0], LAG[1]))

        def copy(self, src, dst, b, q, send, recv, to):
            cut = (b, pl.ds(q * part, part))
            return pltpu.make_async_remote_copy(
                src_ref=src.at[cut], dst_ref=dst.at[cut], send_sem=sends.at[self.sem0 + send],
                recv_sem=recv.at[b * SPLIT + q], device_id=to, device_id_type=pl.DeviceIdType.MESH,
            )

        def head(self):
            m = self.sem0
            move = pltpu.make_async_remote_copy(
                src_ref=meta.at[m + 1], dst_ref=meta.at[m], send_sem=msems.at[m], recv_sem=msems.at[m + 1],
                device_id=self.up, device_id_type=pl.DeviceIdType.MESH,
            )

            @pl.when(self.pos == 0)
            def _():
                meta[m] = jnp.zeros((8, LANES), F32)

            @pl.when(self.pos > 0)
            def _():
                move.wait_recv()

            meta[m + 1] = meta[m] + meta[6]

            @pl.when(self.pos < zr - 1)
            def _():
                move.start()

            return move

        def scan(self, b):
            _, _, a = rates(b)
            g = decay_of(meta[6], a)
            for q in range(SPLIT):
                cut = (b, pl.ds(q * part, part))
                move = self.copy(self.out, self.recv, b, q, 0, self.recv_sem, self.up)

                @pl.when(self.pos > 0)
                def _():
                    move.wait_recv()
                    self.out[cut] = self.out[cut] + g * self.recv[cut]

                @pl.when(self.pos == 0)
                def _():
                    self.recv[cut] = jnp.zeros((part, LANES), F32)

                @pl.when(self.pos < zr - 1)
                def _():
                    move.start()

        def take(self, b):
            _, _, a = rates(b)
            for q in range(SPLIT):
                cut = (b, pl.ds(q * part, part))
                onward = self.copy(self.carry, self.carry, b, q, 1, self.carry_sem, self.down)

                @pl.when(self.row > 0)
                def _():
                    onward.wait_recv()

                    @pl.when(self.pos > 0)
                    def _():
                        onward.start()

                @pl.when((self.pos == zr - 1) & (self.row < xr - 1))
                def _():
                    @pl.when(self.row > 0)
                    def _():
                        self.out[cut] = self.out[cut] + decay_of(meta[self.sem0 + 1], a) * self.carry[cut]

                    self.copy(self.out, self.carry, b, q, 0, self.carry_sem, self.across).start()

                @pl.when(self.row > 0)
                def _():
                    self.recv[cut] = self.recv[cut] + decay_of(meta[self.sem0], a) * self.carry[cut]

        def finish(self, move):
            @pl.when(self.pos < zr - 1)
            def _():
                move.wait_send()

            whole = lambda src, send, recv: pltpu.make_async_remote_copy(
                src_ref=src, dst_ref=src, send_sem=sends.at[self.sem0 + send], recv_sem=recv.at[0],
                device_id=self.up, device_id_type=pl.DeviceIdType.MESH,
            )

            @pl.when((self.pos < zr - 1) | (self.row < xr - 1))
            def _():
                whole(self.out, 0, self.recv_sem).wait_send()

            @pl.when((self.row > 0) & (self.pos > 0))
            def _():
                whole(self.carry, 1, self.carry_sem).wait_send()

        def run(self, make, beside, then):
            def step(i, carry):
                @pl.when(i < nb)
                def _():
                    make(i)
                    self.scan(i)
                    beside(i)

                @pl.when(i >= self.lag)
                def _():
                    self.take(i - self.lag)
                    then(i - self.lag)

                return carry

            lax.fori_loop(0, nb + self.lag, step, 0)

    fwd = Pass(zi, xi, z_at(1), z_at(zr - 1), x_at(1), s_st, p_st, k_st, f_recv, f_carry, 0)
    bwd = Pass(zr - 1 - zi, xr - 1 - xi, z_at(zr - 1), z_at(1), x_at(xr - 1), d_st, r_st, q_st, b_recv, b_carry, 2)

    def block_state(b):
        _, _, a = rates(b)
        u = (x[:, lanes(b)].astype(F32) * (jnp.exp(-a * cols[1]) * cols[2])).astype(BF16)
        ub[:, lanes(b)] = u
        s_st[b] = mm(bt[...], u)

    def scores_of(b):
        a0, a1, _ = rates(b)
        gap, cbd = tab[0], tab[1]
        e0, e1 = jnp.exp(-a0 * gap), jnp.exp(-a1 * gap)
        both = jnp.concatenate([(cbd * e0).astype(BF16), (cbd * e1).astype(BF16)], axis=1)
        return e0, e1, both

    def inside(b):
        _, _, both = scores_of(b)
        mix[:, lanes(b)] = mm(both, pair(b)) + skip_row(b) * x[:, lanes(b)].astype(F32)

    def mixture(b):
        _, _, a = rates(b)
        at = lanes(b)
        state = p_st[b].astype(BF16)
        inter[b] = state
        e = mm(c_mat_ref[...], state)
        ebuf[:, at] = e
        m = mix[:, at] + jnp.exp(-a * cols[0]) * cols[3] * e
        mix[:, at] = m
        zf = z[:, at].astype(F32)
        gated = m * (zf / (1.0 + jnp.exp(-zf)))
        gg = gated * gains[:, at]
        acc[0] += gated * gated
        acc[1] += gg * gg
        acc[2] += gg * tg[:, at].astype(F32)

    c_mat_ref, b_mat_ref = ck, bk

    pl.semaphore_wait(barrier, len(peers))
    first = fwd.head()
    fwd.run(block_state, inside, mixture)

    squares = jnp.sum(acc[0], axis=1, keepdims=True)
    r_col = lax.rsqrt(squares * (1.0 / width) + 1e-5)
    coef = r_col * r_col * r_col * (1.0 / width) * (
        r_col * jnp.sum(acc[1], axis=1, keepdims=True) - jnp.sum(acc[2], axis=1, keepdims=True)
    )
    cols[4] = jnp.broadcast_to(r_col, shape)
    cols[5] = jnp.broadcast_to(coef, shape)

    def direct(b):
        _, _, a = rates(b)
        at = lanes(b)
        m, xf, zf, gain, r = mix[:, at], x[:, at].astype(F32), z[:, at].astype(F32), gains[:, at], cols[4]
        sig = 1.0 / (1.0 + jnp.exp(-zf))
        sg = zf * sig
        gated = m * sg
        unit = gated * r
        miss = unit * gain - tg[:, at].astype(F32)
        dgated = r * (miss * gain) - gated * cols[5]
        dmix = dgated * sg
        de = jnp.exp(-a * cols[0]) * cols[3] * dmix
        deb = de.astype(BF16)
        d_st[b] = mm(ct[...], deb)
        mix[:, at] = dmix
        gz[:, at] = (dgated * m * (sig * (1.0 + zf * (1.0 - sig)))).astype(BF16)
        acc[3, 0:8] += red8(miss * miss)
        ga[b] = red8(miss * unit)
        sa[b] = red8(dmix * xf)
        ra[b] = red8(cols[0] * de * ebuf[:, at])
        acc[4] += mm_nt(deb, inter[b])

    def inside_back(b):
        at = lanes(b)
        e0, e1, both = scores_of(b)
        dmix = mix[:, at]
        dmb = dmix.astype(BF16)
        ds = mm_nt(dmb, pair(b))
        d0, d1 = ds[:, :tok] * e0, ds[:, tok:] * e1
        acc[5] += d0 + d1
        v0, v1 = red8(d0 * tab[2]), red8(d1 * tab[2])
        ra[b] += jnp.where(low, v0 + pltpu.roll(v0, LANES // 2, 1), v1 + pltpu.roll(v1, LANES // 2, 1))
        back = mm_tn(both, dmb)
        dxa[:, at] = jnp.where(low, back[:tok], back[tok:]) + skip_row(b) * dmix

    def state_back(b):
        _, _, a = rates(b)
        at = lanes(b)
        by = r_st[b]
        byb = by.astype(BF16)
        duw = mm(b_mat_ref[...], byb) * (jnp.exp(-a * cols[1]) * cols[2])
        gx[:, at] = (dxa[:, at] + duw).astype(BF16)
        own = meta[6]
        ra[b] += red8(cols[1] * duw * x[:, at].astype(F32)) + red8(by * p_st[b]) * (own[0:1] * decay_of(own, a))
        acc[6] += mm_nt(ub[:, at], byb)

    second = bwd.head()
    bwd.run(direct, inside_back, state_back)

    dcb = (acc[5] * tab[3]).astype(BF16)
    gc[...] = (acc[4] + mm(dcb, bk[...])).astype(BF16)
    gb[...] = (acc[6] + mm_tn(dcb, ck[...])).astype(BF16)

    lane8 = lax.broadcasted_iota(jnp.int32, (8, LANES), 1)
    a_rows = jnp.concatenate([rates(b)[2] for b in range(nb)], axis=0)
    halves = lambda rows: (
        jnp.sum(jnp.where(low, rows, 0.0), axis=1, keepdims=True),
        jnp.sum(jnp.where(low, 0.0, rows), axis=1, keepdims=True),
    )
    packed = jnp.where(lane8 == 127, jnp.broadcast_to(0.5 * jnp.sum(acc[3, 0:8], axis=1, keepdims=True), (8, LANES)), 0.0)
    for base, rows in ((0, ra[...].sum(axis=1) * -a_rows), (64, sa[...].sum(axis=1))):
        h0, h1 = halves(rows)
        for g in range(nb // 8):
            cut = slice(8 * g, 8 * g + 8)
            packed += jnp.where(lane8 == base + 2 * g, h0[cut], 0.0) + jnp.where(lane8 == base + 2 * g + 1, h1[cut], 0.0)
    total = jnp.concatenate([ga[...].sum(axis=1), packed], axis=0)

    for buf, mine, n, at, ss, rs in ((arz, zi, zr, z_at, z_ss, z_rs), (arx, xi, xr, x_at, x_ss, x_rs), (ard, dpi, dpn, d_at, d_ss, d_rs)):
        buf[mine] = total

        def hop(k, slot):
            return pltpu.make_async_remote_copy(
                src_ref=buf.at[slot], dst_ref=buf.at[slot], send_sem=ss.at[k], recv_sem=rs.at[k],
                device_id=at(k), device_id_type=pl.DeviceIdType.MESH,
            )

        for k in range(1, n):
            hop(k, mine).start()
        for k in range(1, n):
            hop(k, lax.rem(mine + n - k, n)).wait_recv()
        total = buf[0]
        for k in range(1, n):
            total = total + buf[k]
        for k in range(1, n):
            hop(k, mine).wait_send()
    red[...] = total * (1.0 / rows_total)
    fwd.finish(first)
    bwd.finish(second)


def shards(mesh, inputs, gates, keys_b, reads_c, step_codes, seg_starts, targets, log_rates, skips, gains):
    tok, width = inputs.shape[1:]
    nb = width // LANES
    seq, dpn = mesh.shape["seq"], mesh.shape["dp"]
    zr = min(Z_RING, seq)
    xr = seq // zr
    vmem, smem = pl.BlockSpec(memory_space=pltpu.VMEM), pl.BlockSpec(memory_space=pltpu.SMEM)
    rows = nb + 8
    state = pltpu.VMEM((nb, tok, LANES), F32)
    dma = pltpu.SemaphoreType.DMA
    wide = jax.ShapeDtypeStruct((tok, width), BF16)
    small = jax.ShapeDtypeStruct(keys_b.shape[1:], BF16)
    gx, gz, gb, gc, red = pl.pallas_call(
        functools.partial(kernel, xr, zr, dpn, nb, float(tok * seq * dpn)),
        out_shape=(wide, wide, small, small, jax.ShapeDtypeStruct((rows, LANES), F32)),
        in_specs=[smem] * 2 + [vmem] * 8,
        out_specs=(vmem,) * 5,
        scratch_shapes=[state] * 6
        + [
            pltpu.VMEM((tok, width), F32),
            pltpu.VMEM((tok, width), F32),
            pltpu.VMEM((tok, width), F32),
            pltpu.VMEM((nb, tok, LANES), BF16),
            pltpu.VMEM((tok, width), BF16),
            pltpu.VMEM((6, tok, LANES), F32),
            pltpu.VMEM((4, tok, tok), F32),
            pltpu.VMEM((7, tok, LANES), F32),
            pltpu.VMEM((nb, 8, LANES), F32),
            pltpu.VMEM((nb, 8, LANES), F32),
            pltpu.VMEM((nb, 8, LANES), F32),
            pltpu.VMEM((LANES, tok), BF16),
            pltpu.VMEM((LANES, tok), BF16),
            pltpu.VMEM((7, 8, LANES), F32),
            pltpu.VMEM((zr, rows, LANES), F32),
            pltpu.VMEM((xr, rows, LANES), F32),
            pltpu.VMEM((dpn, rows, LANES), F32),
        ]
        + [dma((nb * SPLIT,))] * 4
        + [dma((4,)), dma((4,)), dma((zr,)), dma((zr,)), dma((xr,)), dma((xr,)), dma((dpn,)), dma((dpn,))],
        compiler_params=pltpu.CompilerParams(
            collective_id=0, has_side_effects=True, vmem_limit_bytes=52 * 1024 * 1024
        ),
        name="mixer",
    )(
        log_rates, skips, inputs[0], gates[0], targets[0], keys_b[0], reads_c[0],
        step_codes, seg_starts, gains.reshape(1, width),
    )
    tail = red[nb:]
    heads = lambda base: tail[:, base : base + nb // 4].reshape(8, nb // 8, 2).transpose(1, 0, 2).reshape(2 * nb)
    return (
        jnp.sum(tail[:, 127]), gx[None], gz[None], gb[None], gc[None],
        heads(0), heads(64), red[:nb].reshape(width),
    )


def solution(mesh):
    wide, line = P("dp", "seq", None), P("dp", "seq")
    return jax.shard_map(
        functools.partial(shards, mesh),
        mesh=mesh,
        in_specs=(wide, wide, wide, wide, line, line, wide, P(), P(), P()),
        out_specs=(P(), wide, wide, wide, wide, P(), P(), P()),
        check_vma=False,
    )
```

time: 1150 us -> 298 us (0.26)
  waiting for transfers between devices: 799 us -> 0 us
  Pallas kernels: 0 us -> 287 us
  other arithmetic: 155 us -> 0.67 us
  blocking collectives: 113 us -> 0 us
  local copies, waits for them, and re-layouts: 38.3 us -> 8.96 us
  matrix products: 23.1 us -> 0 us
  between operations: 17.7 us -> 0.69 us
    all_gather x2 -> x0, waiting for transfers between devices: 799 us -> none  [prefix(): everything = jax.tree.map(lambda part: lax.all_gather(part, axis), shard)]
    pallas_call x0 -> x1, Pallas kernels: none -> 287 us  [shards(): pl.pallas_call(functools.partial(kernel, xr, zr, dpn, nb, float(tok * seq...]
    select_n x64 -> x0, other arithmetic: 133 us -> none  [hop(): return jax.tree.map(lambda a, b: jnp.where(reached, a, b), new, before)]
    psum x1 -> x0, blocking collectives: 75.3 us -> none  [shards(): lax.psum((loss_here, grad_rate, grad_skip, grad_gain), ('dp', 'seq'))]
    all_gather x1 -> x0, blocking collectives: 37.4 us -> none  [prefix(): everything = jax.tree.map(lambda part: lax.all_gather(part, axis), shard)]
    dot_general x12 -> x0, matrix products: 23.1 us -> none  [the longest x3 9.82 us: local_output(): jnp.dot(incoming.reshape(inner_width, -1), reads_c.astype(jnp.float32).T,...]
    mul x65 -> x0, local copies, waits for them, and re-layouts: 21.6 us -> none  [the longest x64 21.4 us: combine_pair(): later[0][:, :, None, None] * earlier[1] + later[1]]
    reduce_sum x9 -> x1, other arithmetic: 13.2 us -> 0.67 us  [shards(): jnp.sum(tail[:, 127])]
  transfers between devices with their start and end apart: 2 -> 0, of which waited for: 2 -> 0; matrix products, arithmetic and copies ran while one was open for 2% -> 0% of each run, Pallas kernels for 0% -> 0%
where the time goes in v1:
time: 298 us
  Pallas kernels  287 us (96%)
  local copies, waits for them, and re-layouts  8.96 us (3%)
    pallas_call x1, Pallas kernels, shards(): pl.pallas_call(functools.partial(kernel, xr, zr, dpn, nb, float(tok * seq...  287 us
    unnamed x20, local copies, waits for them, and re-layouts  6.7 us

profile of v1, /device:TPU:1, one launch (start us, length us, event | category | flops | bytes accessed | tf_op | source)
XLA Modules:
  0.0 297.8 jit_solution(3089710733188405864)
XLA Ops:
  0.6 0.0 copy-start.6
  0.6 0.0 copy-start.3
  0.7 0.6 copy-done.6
  1.3 0.0 copy-done.3
  1.3 0.0 copy-done.4
  1.3 0.0 copy-done.5
  1.3 0.8 copy-done
  2.1 0.8 copy-done.1
  2.9 0.7 copy-done.2
  3.6 287.5 %mixer.1 = (bf16[128,4096]{1,0:T(8,128)(2,1)S(1)}, bf16[128,4096]{1,0:T(8,128)(2,1)}, bf16[128,128]{1,0:T(8,128)(2,1)S(1)}, bf16[128,128]{1,0:T(8,128)(2,1)S(1)}, f32[40,128]{1,0:T(8,128)S(1)}) custom-call(f32[64]{0:T(128)S(1)} %copy-done.3, f32[64]{0:T(128)S(1)} %copy-done.4, bf16[128,4096]{1,0:T(8,128)(2,1)} %bitcast.25, bf16[128,4096]{1,0:T(8,128)(2,1)} %bitcast.26, ...), custom_call_target="tpu_custom_call" | custom-call | tf_op jit(solution)/shard_map/mixer/pallas_call | solution.py:384
  291.1 0.1 fusion
  291.1 0.1 copy.22
  291.2 0.1 copy.23
  291.3 0.6 reshape.36
  291.9 0.1 copy.24
  292.0 0.1 copy.25
  292.1 0.6 reshape.38
  292.7 0.6 slice_bitcast_fusion
  293.3 0.7 slice_reduce_fusion
  294.0 1.0 copy.30
  295.0 0.6 copy-done.7
  295.6 1.0 copy.31
  296.6 0.6 copy.32
  297.2 0.6 copy.33
  (6 shorter events, 0.0 us)
Async XLA Ops:
  0.6 0.7 copy-start.6
  0.6 0.7 copy-start.3
  0.7 0.7 copy-start.4
  0.7 0.7 copy-start.5
  1.3 0.8 copy-start
  2.1 0.8 copy-start.1
  2.9 0.7 copy-start.2
  294.0 1.6 copy-start.7

commit v2 on v1

--- a/solution.py
+++ b/solution.py
@@ -10,8 +10,8 @@
 F32, BF16 = jnp.float32, jnp.bfloat16
 LANES = 128
 Z_RING = 8
-SPLIT = 2
-LAG = (9, 8)
+SPLIT = 4
+LAG = (20, 8)
 
 
 def red8(v):
@@ -32,13 +32,15 @@
 
 def kernel(
     xr, zr, dpn, nb, rows_total,
-    lr, sk, x, z, tg, bk, ck, codes, segs, gains,
-    gx, gz, gb, gc, red,
+    lr, sk, x_in, z_in, tg_in, bk, ck, codes, segs, gains,
+    gx, gz, gb, gc, red, red_rates,
+    x, z, tg,
     s_st, p_st, k_st, d_st, r_st, q_st,
     mix, ebuf, dxa, inter, ub,
-    cols, tab, acc, ga, sa, ra, bt, ct, meta, arz, arx, ard,
-    f_recv, f_carry, b_recv, b_carry, sends, msems,
-    z_ss, z_rs, x_ss, x_rs, d_ss, d_rs,
+    cols, tab, acc, ga, sa, ra, bt, ct, meta,
+    wide_bufs, rate_bufs,
+    f_recv, f_carry, b_recv, b_carry, sends, msems, local,
+    wide_sems, rate_sems,
 ):
     tok = x.shape[0]
     width = nb * LANES
@@ -52,6 +54,10 @@
     peers = [z_at(k) for k in range(1, zr)] + [x_at(k) for k in range(1, xr)] + [d_at(k) for k in range(1, dpn)]
     for peer in peers:
         pl.semaphore_signal(barrier, inc=1, device_id=peer, device_id_type=pl.DeviceIdType.MESH)
+
+    loads = [pltpu.make_async_copy(src, dst, local.at[i]) for i, (src, dst) in enumerate(((x_in, x), (z_in, z), (tg_in, tg)))]
+    for load in loads:
+        load.start()
 
     t_i = lax.broadcasted_iota(jnp.int32, (tok, tok), 0)
     s_i = lax.broadcasted_iota(jnp.int32, (tok, tok), 1)
@@ -212,13 +218,18 @@
             def _():
                 whole(self.carry, 1, self.carry_sem).wait_send()
 
-        def run(self, make, beside, then):
+        def run(self, make, beside, then, made=None):
             def step(i, carry):
                 @pl.when(i < nb)
                 def _():
                     make(i)
                     self.scan(i)
                     beside(i)
+
+                if made is not None:
+                    @pl.when(i == nb - 1)
+                    def _():
+                        made()
 
                 @pl.when(i >= self.lag)
                 def _():
@@ -267,6 +278,8 @@
 
     c_mat_ref, b_mat_ref = ck, bk
 
+    for load in loads:
+        load.wait()
     pl.semaphore_wait(barrier, len(peers))
     first = fwd.head()
     fwd.run(block_state, inside, mixture)
@@ -325,48 +338,89 @@
         ra[b] += red8(cols[1] * duw * x[:, at].astype(F32)) + red8(by * p_st[b]) * (own[0:1] * decay_of(own, a))
         acc[6] += mm_nt(ub[:, at], byb)
 
+    lane8 = lax.broadcasted_iota(jnp.int32, (8, LANES), 1)
+    row8 = lax.broadcasted_iota(jnp.int32, (8, LANES), 0)
+
+    def by_head(rows):
+        h0 = jnp.sum(jnp.where(low, rows, 0.0), axis=1, keepdims=True)
+        h1 = jnp.sum(jnp.where(low, 0.0, rows), axis=1, keepdims=True)
+        tile = jnp.zeros((8, LANES), F32)
+        for g in range(nb // 8):
+            cut, lane = slice(8 * g, 8 * g + 8), 16 * g + 2 * row8
+            tile += jnp.where(lane8 == lane, h0[cut], 0.0) + jnp.where(lane8 == lane + 1, h1[cut], 0.0)
+        return tile
+
+    class Stage:
+        def __init__(self, buf, sems, axis):
+            self.buf, self.ss, self.rs = buf, sems[0], sems[1]
+            self.mine, self.n, self.at = ((zi, zr, z_at), (xi, xr, x_at), (dpi, dpn, d_at))[axis]
+
+        def hop(self, k, slot):
+            return pltpu.make_async_remote_copy(
+                src_ref=self.buf.at[slot], dst_ref=self.buf.at[slot], send_sem=self.ss.at[k], recv_sem=self.rs.at[k],
+                device_id=self.at(k), device_id_type=pl.DeviceIdType.MESH,
+            )
+
+        def start(self, total):
+            self.buf[self.mine] = total
+            for k in range(1, self.n):
+                self.hop(k, self.mine).start()
+
+        def result(self):
+            for k in range(1, self.n):
+                self.hop(k, lax.rem(self.mine + self.n - k, self.n)).wait_recv()
+            total = self.buf[0]
+            for k in range(1, self.n):
+                total = total + self.buf[k]
+            return total
+
+        def close(self):
+            for k in range(1, self.n):
+                self.hop(k, self.mine).wait_send()
+
+    w_stage = [Stage(wide_bufs[i], wide_sems[i], i) for i in range(3)]
+    r_stage = [Stage(rate_bufs[i], rate_sems[i], i) for i in range(3)]
+
+    def early_sums():
+        lost = 0.5 * jnp.sum(acc[3, 0:8], axis=1, keepdims=True)
+        tile = by_head(sa[...].sum(axis=1)) + jnp.where(lane8 == LANES - 1, lost, 0.0)
+        w_stage[0].start(jnp.concatenate([ga[...].sum(axis=1), tile], axis=0))
+
     second = bwd.head()
-    bwd.run(direct, inside_back, state_back)
-
+    bwd.run(direct, inside_back, state_back, early_sums)
+
+    a_rows = jnp.concatenate([rates(b)[2] for b in range(nb)], axis=0)
+    r_stage[0].start(by_head(ra[...].sum(axis=1) * -a_rows))
+    w_stage[1].start(w_stage[0].result())
     dcb = (acc[5] * tab[3]).astype(BF16)
     gc[...] = (acc[4] + mm(dcb, bk[...])).astype(BF16)
     gb[...] = (acc[6] + mm_tn(dcb, ck[...])).astype(BF16)
-
-    lane8 = lax.broadcasted_iota(jnp.int32, (8, LANES), 1)
-    a_rows = jnp.concatenate([rates(b)[2] for b in range(nb)], axis=0)
-    halves = lambda rows: (
-        jnp.sum(jnp.where(low, rows, 0.0), axis=1, keepdims=True),
-        jnp.sum(jnp.where(low, 0.0, rows), axis=1, keepdims=True),
-    )
-    packed = jnp.where(lane8 == 127, jnp.broadcast_to(0.5 * jnp.sum(acc[3, 0:8], axis=1, keepdims=True), (8, LANES)), 0.0)
-    for base, rows in ((0, ra[...].sum(axis=1) * -a_rows), (64, sa[...].sum(axis=1))):
-        h0, h1 = halves(rows)
-        for g in range(nb // 8):
-            cut = slice(8 * g, 8 * g + 8)
-            packed += jnp.where(lane8 == base + 2 * g, h0[cut], 0.0) + jnp.where(lane8 == base + 2 * g + 1, h1[cut], 0.0)
-    total = jnp.concatenate([ga[...].sum(axis=1), packed], axis=0)
-
-    for buf, mine, n, at, ss, rs in ((arz, zi, zr, z_at, z_ss, z_rs), (arx, xi, xr, x_at, x_ss, x_rs), (ard, dpi, dpn, d_at, d_ss, d_rs)):
-        buf[mine] = total
-
-        def hop(k, slot):
-            return pltpu.make_async_remote_copy(
-                src_ref=buf.at[slot], dst_ref=buf.at[slot], send_sem=ss.at[k], recv_sem=rs.at[k],
-                device_id=at(k), device_id_type=pl.DeviceIdType.MESH,
-            )
-
-        for k in range(1, n):
-            hop(k, mine).start()
-        for k in range(1, n):
-            hop(k, lax.rem(mine + n - k, n)).wait_recv()
-        total = buf[0]
-        for k in range(1, n):
-            total = total + buf[k]
-        for k in range(1, n):
-            hop(k, mine).wait_send()
-    red[...] = total * (1.0 / rows_total)
+    r_stage[1].start(r_stage[0].result())
+    w_stage[2].start(w_stage[1].result())
+    r_stage[2].start(r_stage[1].result())
+    red[...] = w_stage[2].result() * (1.0 / rows_total)
     fwd.finish(first)
     bwd.finish(second)
+    for stage in w_stage + r_stage[:2]:
+        stage.close()
+    red_rates[...] = r_stage[2].result() * (1.0 / rows_total)
+    r_stage[2].close()
+
+
+def hand_over(nb, gx, gz, gb, gc, red, red_rates, gx_out, gz_out, gb_out, gc_out, loss, rate, skip, gain, sems):
+    moves = [pltpu.make_async_copy(a, b, sems.at[i]) for i, (a, b) in enumerate(((gx, gx_out), (gz, gz_out)))]
+    for move in moves:
+        move.start()
+    gb_out[...] = gb[...]
+    gc_out[...] = gc[...]
+    for b in range(nb):
+        gain[:, b * LANES : (b + 1) * LANES] = red[b : b + 1, :]
+    tail = jnp.sum(red[nb:, :], axis=0, keepdims=True)
+    loss[...] = tail[:, LANES - 1 :]
+    skip[...] = tail[:, : 2 * nb]
+    rate[...] = jnp.sum(red_rates[...], axis=0, keepdims=True)[:, : 2 * nb]
+    for move in moves:
+        move.wait()
 
 
 def shards(mesh, inputs, gates, keys_b, reads_c, step_codes, seg_starts, targets, log_rates, skips, gains):
@@ -376,23 +430,27 @@
     zr = min(Z_RING, seq)
     xr = seq // zr
     vmem, smem = pl.BlockSpec(memory_space=pltpu.VMEM), pl.BlockSpec(memory_space=pltpu.SMEM)
+    hbm = pl.BlockSpec(memory_space=pltpu.HBM)
     rows = nb + 8
     state = pltpu.VMEM((nb, tok, LANES), F32)
     dma = pltpu.SemaphoreType.DMA
-    wide = jax.ShapeDtypeStruct((tok, width), BF16)
-    small = jax.ShapeDtypeStruct(keys_b.shape[1:], BF16)
-    gx, gz, gb, gc, red = pl.pallas_call(
+    counts = (zr, xr, dpn)
+    of = jax.ShapeDtypeStruct
+    wide, small = of((tok, width), BF16), of(keys_b.shape[1:], BF16)
+    flat, half = pltpu.VMEM((tok, width), F32), pltpu.VMEM((tok, width), BF16)
+    results = pl.pallas_call(
         functools.partial(kernel, xr, zr, dpn, nb, float(tok * seq * dpn)),
-        out_shape=(wide, wide, small, small, jax.ShapeDtypeStruct((rows, LANES), F32)),
-        in_specs=[smem] * 2 + [vmem] * 8,
-        out_specs=(vmem,) * 5,
-        scratch_shapes=[state] * 6
+        out_shape=(wide, wide, small, small, of((rows, LANES), F32), of((8, LANES), F32)),
+        in_specs=[smem] * 2 + [hbm] * 3 + [vmem] * 5,
+        out_specs=(vmem,) * 6,
+        scratch_shapes=[half] * 3
+        + [state] * 6
         + [
-            pltpu.VMEM((tok, width), F32),
-            pltpu.VMEM((tok, width), F32),
-            pltpu.VMEM((tok, width), F32),
+            flat,
+            flat,
+            flat,
             pltpu.VMEM((nb, tok, LANES), BF16),
-            pltpu.VMEM((tok, width), BF16),
+            half,
             pltpu.VMEM((6, tok, LANES), F32),
             pltpu.VMEM((4, tok, tok), F32),
             pltpu.VMEM((7, tok, LANES), F32),
@@ -402,25 +460,31 @@
             pltpu.VMEM((LANES, tok), BF16),
             pltpu.VMEM((LANES, tok), BF16),
             pltpu.VMEM((7, 8, LANES), F32),
-            pltpu.VMEM((zr, rows, LANES), F32),
-            pltpu.VMEM((xr, rows, LANES), F32),
-            pltpu.VMEM((dpn, rows, LANES), F32),
+            [pltpu.VMEM((n, rows, LANES), F32) for n in counts],
+            [pltpu.VMEM((n, 8, LANES), F32) for n in counts],
         ]
         + [dma((nb * SPLIT,))] * 4
-        + [dma((4,)), dma((4,)), dma((zr,)), dma((zr,)), dma((xr,)), dma((xr,)), dma((dpn,)), dma((dpn,))],
+        + [dma((4,)), dma((4,)), dma((3,))]
+        + [[[dma((n,)), dma((n,))] for n in counts] for _ in range(2)],
         compiler_params=pltpu.CompilerParams(
-            collective_id=0, has_side_effects=True, vmem_limit_bytes=52 * 1024 * 1024
+            collective_id=0, has_side_effects=True, vmem_limit_bytes=56 * 1024 * 1024
         ),
         name="mixer",
     )(
         log_rates, skips, inputs[0], gates[0], targets[0], keys_b[0], reads_c[0],
         step_codes, seg_starts, gains.reshape(1, width),
     )
-    tail = red[nb:]
-    heads = lambda base: tail[:, base : base + nb // 4].reshape(8, nb // 8, 2).transpose(1, 0, 2).reshape(2 * nb)
+    line = of((1, 2 * nb), F32)
+    gx, gz, gb, gc, loss, rate, skip, gain = pl.pallas_call(
+        functools.partial(hand_over, nb),
+        out_shape=(wide, wide, small, small, of((1, 1), F32), line, line, of((1, width), F32)),
+        in_specs=[vmem] * 6,
+        out_specs=(hbm,) * 2 + (vmem,) * 6,
+        scratch_shapes=[dma((2,))],
+        name="hand_over",
+    )(*results)
     return (
-        jnp.sum(tail[:, 127]), gx[None], gz[None], gb[None], gc[None],
-        heads(0), heads(64), red[:nb].reshape(width),
+        loss[0, 0], gx[None], gz[None], gb[None], gc[None], rate[0], skip[0], gain[0],
     )
 
 

time: 298 us -> 209 us (0.70)
  Pallas kernels: 287 us -> 208 us
  local copies, waits for them, and re-layouts: 8.96 us -> 0 us
    pallas_call x1, Pallas kernels: 287 us -> 204 us  [shards(): pl.pallas_call(functools.partial(kernel, xr, zr, dpn, nb, float(tok * seq...]
    unnamed x20 -> x0, local copies, waits for them, and re-layouts: 6.7 us -> none
    pallas_call x0 -> x1, Pallas kernels: none -> 3.54 us  [shards(): pl.pallas_call(functools.partial(hand_over, nb), out_shape=(wide, wide, s...]
where the time goes in v2:
time: 209 us
  Pallas kernels  208 us (100%)
    pallas_call x1, Pallas kernels, shards(): pl.pallas_call(functools.partial(kernel, xr, zr, dpn, nb, float(tok * seq...  204 us

profile of v2, /device:TPU:1, one launch (start us, length us, event | category | flops | bytes accessed | tf_op | source)
XLA Modules:
  0.0 208.7 jit_solution(2889769295115717345)
XLA Ops:
  0.6 204.5 %mixer.1 = (bf16[128,4096]{1,0:T(8,128)(2,1)}, bf16[128,4096]{1,0:T(8,128)(2,1)}, bf16[128,128]{1,0:T(8,128)(2,1)}, bf16[128,128]{1,0:T(8,128)(2,1)}, f32[40,128]{1,0:T(8,128)}, /*index=5*/f32[8,128]{1,0:T(8,128)}) custom-call(f32[64]{0:T(128)} %lr.1, f32[64]{0:T(128)} %sk.1, bf16[128,4096]{1,0:T(8,128)(2,1)} %bitcast.14, bf16[128,4096]{1,0:T(8,128)(2,1)} %bitcast.15, ...), custom_call_target="tpu_custom_call" | custom-call | tf_op jit(solution)/shard_map/mixer/pallas_call | solution.py:441
  205.1 3.5 %hand_over.1 = (bf16[128,4096]{1,0:T(8,128)(2,1)}, bf16[128,4096]{1,0:T(8,128)(2,1)}, bf16[128,128]{1,0:T(8,128)(2,1)}, bf16[128,128]{1,0:T(8,128)(2,1)}, f32[1,...) custom-call(bf16[128,4096]{1,0:T(8,128)(2,1)} %get-tuple-element.22.gx, ...), custom_call_target="tpu_custom_call" | custom-call | tf_op jit(solution)/shard_map/hand_over/pallas_call | solution.py:478

commit v3 on v2

--- a/solution.py
+++ b/solution.py
@@ -10,8 +10,8 @@
 F32, BF16 = jnp.float32, jnp.bfloat16
 LANES = 128
 Z_RING = 8
-SPLIT = 4
-LAG = (20, 8)
+SPLIT = 2
+HOP = (21, 8)
 
 
 def red8(v):
@@ -35,12 +35,12 @@
     lr, sk, x_in, z_in, tg_in, bk, ck, codes, segs, gains,
     gx, gz, gb, gc, red, red_rates,
     x, z, tg,
-    s_st, p_st, k_st, d_st, r_st, q_st,
+    f_out, p_st, f_carry, f_part, b_out, r_st, b_carry, b_part,
     mix, ebuf, dxa, inter, ub,
-    cols, tab, acc, ga, sa, ra, bt, ct, meta,
+    cols, tab, acc, ga, sa, ra, bt, ct, meta, row_meta,
     wide_bufs, rate_bufs,
-    f_recv, f_carry, b_recv, b_carry, sends, msems, local,
-    wide_sems, rate_sems,
+    recv_sems, sends, local,
+    wide_sems, rate_sems, meta_sems,
 ):
     tok = x.shape[0]
     width = nb * LANES
@@ -88,7 +88,7 @@
     bt[...], ct[...] = b_mat.astype(F32).T.astype(BF16), c_mat.astype(F32).T.astype(BF16)
     end_dt = jnp.broadcast_to(cum_end * (1.0 / 64.0), (1, LANES))
     broken = jnp.broadcast_to((seg_end > 0.0).astype(F32), (1, LANES))
-    meta[6] = jnp.where(
+    meta[10] = jnp.where(
         lax.broadcasted_iota(jnp.int32, (8, LANES), 0) == 0, end_dt,
         jnp.where(lax.broadcasted_iota(jnp.int32, (8, LANES), 0) == 1, broken, 0.0),
     )
@@ -117,137 +117,353 @@
 
     part = tok // SPLIT
 
+    class Stage:
+        def __init__(self, buf, sems, axis):
+            self.buf, self.ss, self.rs = buf, sems[0], sems[1]
+            self.mine, self.n, self.at = ((zi, zr, z_at), (xi, xr, x_at), (dpi, dpn, d_at))[axis]
+
+        def hop(self, k, slot):
+            return pltpu.make_async_remote_copy(
+                src_ref=self.buf.at[slot], dst_ref=self.buf.at[slot], send_sem=self.ss.at[k], recv_sem=self.rs.at[k],
+                device_id=self.at(k), device_id_type=pl.DeviceIdType.MESH,
+            )
+
+        def start(self, total):
+            self.buf[self.mine] = total
+            for k in range(1, self.n):
+                self.hop(k, self.mine).start()
+
+        def result(self):
+            for k in range(1, self.n):
+                self.hop(k, lax.rem(self.mine + self.n - k, self.n)).wait_recv()
+            total = self.buf[0]
+            for k in range(1, self.n):
+                total = total + self.buf[k]
+            return total
+
+        def close(self):
+            for k in range(1, self.n):
+                self.hop(k, self.mine).wait_send()
+
+    half, mid = nb // 2, zr // 2
+    ticks = lambda hops: lax.div(hops * HOP[0], HOP[1])
+
     class Pass:
-        def __init__(self, pos, row, up, down, across, out, recv, carry, recv_sem, carry_sem, sem0):
-            self.pos, self.row, self.up, self.down, self.across = pos, row, up, down, across
-            self.out, self.recv, self.carry = out, recv, carry
-            self.recv_sem, self.carry_sem, self.sem0 = recv_sem, carry_sem, sem0
-            self.lag = jnp.where(row == 0, 0, lax.div((2 * (zr - 1) + row - 2 * pos) * LAG[0], LAG[1]))
-
-        def copy(self, src, dst, b, q, send, recv, to):
+        def __init__(self, backward, out, recv, carry, partial):
+            self.p = zr - 1 - zi if backward else zi
+            self.r = xr - 1 - xi if backward else xi
+            self.up, self.down = (z_at(zr - 1), z_at(1)) if backward else (z_at(1), z_at(zr - 1))
+            self.across = x_at(xr - 1) if backward else x_at(1)
+            self.out, self.recv, self.carry, self.part = out, recv, carry, partial
+            self.base, self.backward = 5 * backward, backward
+            self.sems = recv_sems[3 * backward : 3 * backward + 3]
+            p, r = self.p, self.r
+            self.low, self.high = p < mid, p >= mid
+            self.first = [
+                ticks(jnp.where(p < mid, p, zr - 1 - p)),
+                ticks(jnp.where(p < mid, mid - 1 - p, p - mid)),
+            ]
+            self.second = [
+                ticks(jnp.where(p < mid, jnp.where(r > 0, zr + r - p, p), r + p)),
+                ticks(jnp.where(p < mid, mid + r + p, mid + r + zr - p)),
+            ]
+
+        def place_meta(self):
+            slots = range(zr)
+            at = lambda slot: zr - 1 - slot if self.backward else slot
+            same = lambda q: self.low if q < mid else self.high
+            rules = (
+                lambda q: same(q) & (q < self.p),
+                lambda q: same(q) & (q > self.p),
+                lambda q: q < mid,
+                lambda q: q >= mid,
+                lambda q: True,
+            )
+            for n, rule in enumerate(rules):
+                total = jnp.zeros((8, LANES), F32)
+                for slot in slots:
+                    total = total + jnp.where(rule(at(slot)), 1.0, 0.0) * row_meta[slot]
+                meta[self.base + n] = total
+
+        def decay(self, n, b):
+            return decay_of(meta[self.base + n], rates(b)[2])
+
+        def own(self, b):
+            return decay_of(meta[10], rates(b)[2])
+
+        def copy(self, src, dst, b, q, send, kind, to):
             cut = (b, pl.ds(q * part, part))
             return pltpu.make_async_remote_copy(
-                src_ref=src.at[cut], dst_ref=dst.at[cut], send_sem=sends.at[self.sem0 + send],
-                recv_sem=recv.at[b * SPLIT + q], device_id=to, device_id_type=pl.DeviceIdType.MESH,
+                src_ref=src.at[cut], dst_ref=dst.at[cut], send_sem=sends.at[send],
+                recv_sem=self.sems[kind].at[b * SPLIT + q], device_id=to, device_id_type=pl.DeviceIdType.MESH,
             )
 
-        def head(self):
-            m = self.sem0
-            move = pltpu.make_async_remote_copy(
-                src_ref=meta.at[m + 1], dst_ref=meta.at[m], send_sem=msems.at[m], recv_sem=msems.at[m + 1],
-                device_id=self.up, device_id_type=pl.DeviceIdType.MESH,
-            )
-
-            @pl.when(self.pos == 0)
-            def _():
-                meta[m] = jnp.zeros((8, LANES), F32)
-
-            @pl.when(self.pos > 0)
-            def _():
-                move.wait_recv()
-
-            meta[m + 1] = meta[m] + meta[6]
-
-            @pl.when(self.pos < zr - 1)
-            def _():
-                move.start()
-
-            return move
-
-        def scan(self, b):
-            _, _, a = rates(b)
-            g = decay_of(meta[6], a)
+        def moves(self, s, b, q):
+            sem = 6 * self.backward + 3 * s
+            out, recv, carry, partial = self.out, self.recv, self.carry, self.part
+            wait_recv = lambda: self.copy(recv, recv, b, q, sem, 0, self.up).wait_recv()
+            wait_carry = lambda: self.copy(carry, carry, b, q, sem, 1, self.up).wait_recv()
+            wait_part = lambda: self.copy(partial, partial, b, q, sem, 2, self.up).wait_recv()
+            send_up = lambda: self.copy(out, recv, b, q, sem, 0, self.up).start()
+            carry_down = lambda: self.copy(carry, carry, b, q, sem + 1, 1, self.down).start()
+            part_down = lambda: self.copy(partial, partial, b, q, sem + 2, 2, self.down).start()
+            return wait_recv, wait_carry, wait_part, send_up, carry_down, part_down
+
+        def middle_first(self, b):
+            p, r = self.p, self.r
+            g, above = self.own(b), self.decay(1, b)
             for q in range(SPLIT):
                 cut = (b, pl.ds(q * part, part))
-                move = self.copy(self.out, self.recv, b, q, 0, self.recv_sem, self.up)
-
-                @pl.when(self.pos > 0)
-                def _():
-                    move.wait_recv()
-                    self.out[cut] = self.out[cut] + g * self.recv[cut]
-
-                @pl.when(self.pos == 0)
-                def _():
-                    self.recv[cut] = jnp.zeros((part, LANES), F32)
-
-                @pl.when(self.pos < zr - 1)
-                def _():
-                    move.start()
-
-        def take(self, b):
-            _, _, a = rates(b)
+                wait_recv, _, wait_part, send_up, _, part_down = self.moves(0, b, q)
+
+                @pl.when(p < mid)
+                def _():
+                    @pl.when(p > 0)
+                    def _():
+                        wait_recv()
+                        self.out[cut] = self.out[cut] + g * self.recv[cut]
+
+                    @pl.when(p == 0)
+                    def _():
+                        self.recv[cut] = jnp.zeros((part, LANES), F32)
+
+                    send_up()
+
+                @pl.when((p > mid) & (r < xr - 1))
+                def _():
+                    @pl.when(p < zr - 1)
+                    def _():
+                        wait_part()
+                        self.part[cut] = self.part[cut] + above * self.out[cut]
+
+                    @pl.when(p == zr - 1)
+                    def _():
+                        self.part[cut] = self.out[cut]
+
+                    part_down()
+
+        def ends_first(self, b):
+            p, r = self.p, self.r
+            g, above = self.own(b), self.decay(1, b)
             for q in range(SPLIT):
                 cut = (b, pl.ds(q * part, part))
-                onward = self.copy(self.carry, self.carry, b, q, 1, self.carry_sem, self.down)
-
-                @pl.when(self.row > 0)
-                def _():
-                    onward.wait_recv()
-
-                    @pl.when(self.pos > 0)
-                    def _():
-                        onward.start()
-
-                @pl.when((self.pos == zr - 1) & (self.row < xr - 1))
-                def _():
-                    @pl.when(self.row > 0)
-                    def _():
-                        self.out[cut] = self.out[cut] + decay_of(meta[self.sem0 + 1], a) * self.carry[cut]
-
-                    self.copy(self.out, self.carry, b, q, 0, self.carry_sem, self.across).start()
-
-                @pl.when(self.row > 0)
-                def _():
-                    self.recv[cut] = self.recv[cut] + decay_of(meta[self.sem0], a) * self.carry[cut]
-
-        def finish(self, move):
-            @pl.when(self.pos < zr - 1)
-            def _():
-                move.wait_send()
-
-            whole = lambda src, send, recv: pltpu.make_async_remote_copy(
-                src_ref=src, dst_ref=src, send_sem=sends.at[self.sem0 + send], recv_sem=recv.at[0],
-                device_id=self.up, device_id_type=pl.DeviceIdType.MESH,
+                wait_recv, _, wait_part, send_up, _, part_down = self.moves(1, b, q)
+                to_end = lambda: self.copy(self.out, self.carry, b, q, 6 * self.backward + 3, 1, self.up).start()
+
+                @pl.when(p < mid)
+                def _():
+                    @pl.when(p < mid - 1)
+                    def _():
+                        wait_part()
+                        self.part[cut] = self.part[cut] + above * self.out[cut]
+
+                    @pl.when(p == mid - 1)
+                    def _():
+                        self.part[cut] = self.out[cut]
+
+                    @pl.when(p > 0)
+                    def _():
+                        part_down()
+
+                @pl.when(p >= mid)
+                def _():
+                    @pl.when(p > mid)
+                    def _():
+                        wait_recv()
+                        self.out[cut] = self.out[cut] + g * self.recv[cut]
+
+                    @pl.when(p == mid)
+                    def _():
+                        self.recv[cut] = jnp.zeros((part, LANES), F32)
+
+                    @pl.when(p < zr - 1)
+                    def _():
+                        send_up()
+
+                    @pl.when((p == zr - 1) & (r < xr - 1))
+                    def _():
+                        to_end()
+
+        def middle_second(self, b):
+            p, r = self.p, self.r
+            g = self.own(b)
+            for q in range(SPLIT):
+                cut = (b, pl.ds(q * part, part))
+                wait_recv, wait_carry, wait_part, send_up, carry_down, _ = self.moves(0, b, q)
+                onward = lambda: self.copy(self.part, self.carry, b, q, 6 * self.backward + 2, 1, self.across).start()
+
+                @pl.when((p <= mid) & (r > 0))
+                def _():
+                    wait_carry()
+
+                    @pl.when(p > 0)
+                    def _():
+                        carry_down()
+
+                @pl.when((p < mid) & (r > 0))
+                def _():
+                    self.recv[cut] = self.recv[cut] + self.decay(0, b) * self.carry[cut]
+
+                @pl.when(p >= mid)
+                def _():
+                    wait_recv()
+
+                @pl.when(p == mid)
+                def _():
+                    @pl.when(r < xr - 1)
+                    def _():
+                        wait_part()
+                        own = self.part[cut] + self.decay(1, b) * self.out[cut] + self.decay(3, b) * self.recv[cut]
+
+                        @pl.when(r > 0)
+                        def _():
+                            self.part[cut] = own + self.decay(4, b) * self.carry[cut]
+
+                        @pl.when(r == 0)
+                        def _():
+                            self.part[cut] = own
+
+                        onward()
+
+                    @pl.when(r > 0)
+                    def _():
+                        self.recv[cut] = self.recv[cut] + self.decay(2, b) * self.carry[cut]
+
+                @pl.when((p >= mid) & (p < zr - 1))
+                def _():
+                    self.out[cut] = self.out[cut] + g * self.recv[cut]
+                    send_up()
+
+        def ends_second(self, b):
+            p, r = self.p, self.r
+            g = self.own(b)
+            for q in range(SPLIT):
+                cut = (b, pl.ds(q * part, part))
+                wait_recv, wait_carry, _, send_up, carry_down, _ = self.moves(1, b, q)
+                onward = lambda: self.copy(self.carry, self.recv, b, q, 6 * self.backward + 4, 0, self.across).start()
+                to_end = lambda: self.copy(self.part, self.carry, b, q, 6 * self.backward + 5, 1, self.down).start()
+
+                @pl.when((p < mid) & ((p > 0) | (r > 0)))
+                def _():
+                    wait_recv()
+
+                @pl.when((p == 0) & (r == 0))
+                def _():
+                    self.recv[cut] = jnp.zeros((part, LANES), F32)
+
+                @pl.when((p == 0) & (r < xr - 1))
+                def _():
+                    wait_carry()
+                    self.carry[cut] = self.carry[cut] + self.decay(3, b) * self.part[cut] + self.decay(4, b) * self.recv[cut]
+                    onward()
+
+                @pl.when(p < mid - 1)
+                def _():
+                    self.out[cut] = self.out[cut] + g * self.recv[cut]
+                    send_up()
+
+                @pl.when(p == 0)
+                def _():
+                    self.part[cut] = self.part[cut] + self.decay(2, b) * self.recv[cut]
+                    to_end()
+
+                @pl.when(p >= mid)
+                def _():
+                    wait_carry()
+
+                    @pl.when(p > mid)
+                    def _():
+                        carry_down()
+
+                    self.recv[cut] = self.recv[cut] + self.decay(0, b) * self.carry[cut]
+
+        def finish(self):
+            p, r = self.p, self.r
+            sent = (
+                (p < zr - 1),
+                (p <= mid) & (p > 0) & (r > 0),
+                (p >= mid) & (r < xr - 1),
+                (p != mid - 1) & ((p < zr - 1) | (r < xr - 1)),
+                ((p == 0) & (r < xr - 1)) | (p > mid),
+                (p < mid),
             )
-
-            @pl.when((self.pos < zr - 1) | (self.row < xr - 1))
-            def _():
-                whole(self.out, 0, self.recv_sem).wait_send()
-
-            @pl.when((self.row > 0) & (self.pos > 0))
-            def _():
-                whole(self.carry, 1, self.carry_sem).wait_send()
-
-        def run(self, make, beside, then, made=None):
-            def step(i, carry):
-                @pl.when(i < nb)
-                def _():
-                    make(i)
-                    self.scan(i)
-                    beside(i)
-
-                if made is not None:
-                    @pl.when(i == nb - 1)
-                    def _():
-                        made()
-
-                @pl.when(i >= self.lag)
-                def _():
-                    self.take(i - self.lag)
-                    then(i - self.lag)
-
-                return carry
-
-            lax.fori_loop(0, nb + self.lag, step, 0)
-
-    fwd = Pass(zi, xi, z_at(1), z_at(zr - 1), x_at(1), s_st, p_st, k_st, f_recv, f_carry, 0)
-    bwd = Pass(zr - 1 - zi, xr - 1 - xi, z_at(zr - 1), z_at(1), x_at(xr - 1), d_st, r_st, q_st, b_recv, b_carry, 2)
+            for n, did in enumerate(sent):
+                src = (self.out, self.carry, self.part)[n % 3].at[pl.ds(n // 3 * half, half)]
+                move = pltpu.make_async_remote_copy(
+                    src_ref=src, dst_ref=src, send_sem=sends.at[6 * self.backward + n], recv_sem=self.sems[0].at[0],
+                    device_id=self.up, device_id_type=pl.DeviceIdType.MESH,
+                )
+
+                @pl.when(did)
+                def _():
+                    move.wait_send()
+
+        def run(self, make, beside, then, events):
+            def tick(i, _):
+                def early(s, _):
+                    c = i - jnp.where(s == 0, self.first[0], self.first[1])
+
+                    @pl.when((c >= 0) & (c < half))
+                    def _():
+                        b = s * half + c
+                        make(b)
+
+                        @pl.when(s == 0)
+                        def _():
+                            self.middle_first(b)
+
+                        @pl.when(s == 1)
+                        def _():
+                            self.ends_first(b)
+
+                        beside(b)
+
+                    return 0
+
+                def late(s, _):
+                    c = i - jnp.where(s == 0, self.second[0], self.second[1])
+
+                    @pl.when((c >= 0) & (c < half))
+                    def _():
+                        b = s * half + c
+
+                        @pl.when(s == 0)
+                        def _():
+                            self.middle_second(b)
+
+                        @pl.when(s == 1)
+                        def _():
+                            self.ends_second(b)
+
+                        then(b)
+
+                    return 0
+
+                lax.fori_loop(0, 2, early, 0)
+                for when, event in events:
+                    @pl.when(i == when)
+                    def _():
+                        event()
+
+                lax.fori_loop(0, 2, late, 0)
+                return 0
+
+            lax.fori_loop(0, half + jnp.maximum(self.second[0], self.second[1]), tick, 0)
+
+    fwd = Pass(False, f_out, p_st, f_carry, f_part)
+    bwd = Pass(True, b_out, r_st, b_carry, b_part)
+    meta_stage = Stage(row_meta, meta_sems, 0)
+
+    def take_meta():
+        meta_stage.result()
+        fwd.place_meta()
+        bwd.place_meta()
 
     def block_state(b):
         _, _, a = rates(b)
         u = (x[:, lanes(b)].astype(F32) * (jnp.exp(-a * cols[1]) * cols[2])).astype(BF16)
         ub[:, lanes(b)] = u
-        s_st[b] = mm(bt[...], u)
+        f_out[b] = mm(bt[...], u)
 
     def scores_of(b):
         a0, a1, _ = rates(b)
@@ -281,8 +497,8 @@
     for load in loads:
         load.wait()
     pl.semaphore_wait(barrier, len(peers))
-    first = fwd.head()
-    fwd.run(block_state, inside, mixture)
+    meta_stage.start(meta[10])
+    fwd.run(block_state, inside, mixture, [(1, take_meta)])
 
     squares = jnp.sum(acc[0], axis=1, keepdims=True)
     r_col = lax.rsqrt(squares * (1.0 / width) + 1e-5)
@@ -305,7 +521,7 @@
         dmix = dgated * sg
         de = jnp.exp(-a * cols[0]) * cols[3] * dmix
         deb = de.astype(BF16)
-        d_st[b] = mm(ct[...], deb)
+        b_out[b] = mm(ct[...], deb)
         mix[:, at] = dmix
         gz[:, at] = (dgated * m * (sig * (1.0 + zf * (1.0 - sig)))).astype(BF16)
         acc[3, 0:8] += red8(miss * miss)
@@ -334,7 +550,7 @@
         byb = by.astype(BF16)
         duw = mm(b_mat_ref[...], byb) * (jnp.exp(-a * cols[1]) * cols[2])
         gx[:, at] = (dxa[:, at] + duw).astype(BF16)
-        own = meta[6]
+        own = meta[10]
         ra[b] += red8(cols[1] * duw * x[:, at].astype(F32)) + red8(by * p_st[b]) * (own[0:1] * decay_of(own, a))
         acc[6] += mm_nt(ub[:, at], byb)
 
@@ -350,34 +566,6 @@
             tile += jnp.where(lane8 == lane, h0[cut], 0.0) + jnp.where(lane8 == lane + 1, h1[cut], 0.0)
         return tile
 
-    class Stage:
-        def __init__(self, buf, sems, axis):
-            self.buf, self.ss, self.rs = buf, sems[0], sems[1]
-            self.mine, self.n, self.at = ((zi, zr, z_at), (xi, xr, x_at), (dpi, dpn, d_at))[axis]
-
-        def hop(self, k, slot):
-            return pltpu.make_async_remote_copy(
-                src_ref=self.buf.at[slot], dst_ref=self.buf.at[slot], send_sem=self.ss.at[k], recv_sem=self.rs.at[k],
-                device_id=self.at(k), device_id_type=pl.DeviceIdType.MESH,
-            )
-
-        def start(self, total):
-            self.buf[self.mine] = total
-            for k in range(1, self.n):
-                self.hop(k, self.mine).start()
-
-        def result(self):
-            for k in range(1, self.n):
-                self.hop(k, lax.rem(self.mine + self.n - k, self.n)).wait_recv()
-            total = self.buf[0]
-            for k in range(1, self.n):
-                total = total + self.buf[k]
-            return total
-
-        def close(self):
-            for k in range(1, self.n):
-                self.hop(k, self.mine).wait_send()
-
     w_stage = [Stage(wide_bufs[i], wide_sems[i], i) for i in range(3)]
     r_stage = [Stage(rate_bufs[i], rate_sems[i], i) for i in range(3)]
 
@@ -386,8 +574,7 @@
         tile = by_head(sa[...].sum(axis=1)) + jnp.where(lane8 == LANES - 1, lost, 0.0)
         w_stage[0].start(jnp.concatenate([ga[...].sum(axis=1), tile], axis=0))
 
-    second = bwd.head()
-    bwd.run(direct, inside_back, state_back, early_sums)
+    bwd.run(direct, inside_back, state_back, [(half - 1 + jnp.maximum(bwd.first[0], bwd.first[1]), early_sums)])
 
     a_rows = jnp.concatenate([rates(b)[2] for b in range(nb)], axis=0)
     r_stage[0].start(by_head(ra[...].sum(axis=1) * -a_rows))
@@ -399,8 +586,9 @@
     w_stage[2].start(w_stage[1].result())
     r_stage[2].start(r_stage[1].result())
     red[...] = w_stage[2].result() * (1.0 / rows_total)
-    fwd.finish(first)
-    bwd.finish(second)
+    fwd.finish()
+    bwd.finish()
+    meta_stage.close()
     for stage in w_stage + r_stage[:2]:
         stage.close()
     red_rates[...] = r_stage[2].result() * (1.0 / rows_total)
@@ -444,7 +632,7 @@
         in_specs=[smem] * 2 + [hbm] * 3 + [vmem] * 5,
         out_specs=(vmem,) * 6,
         scratch_shapes=[half] * 3
-        + [state] * 6
+        + [state] * 8
         + [
             flat,
             flat,
@@ -459,13 +647,14 @@
             pltpu.VMEM((nb, 8, LANES), F32),
             pltpu.VMEM((LANES, tok), BF16),
             pltpu.VMEM((LANES, tok), BF16),
-            pltpu.VMEM((7, 8, LANES), F32),
+            pltpu.VMEM((11, 8, LANES), F32),
+            pltpu.VMEM((zr, 8, LANES), F32),
             [pltpu.VMEM((n, rows, LANES), F32) for n in counts],
             [pltpu.VMEM((n, 8, LANES), F32) for n in counts],
         ]
-        + [dma((nb * SPLIT,))] * 4
-        + [dma((4,)), dma((4,)), dma((3,))]
-        + [[[dma((n,)), dma((n,))] for n in counts] for _ in range(2)],
+        + [[dma((nb * SPLIT,))] * 6, dma((12,)), dma((3,))]
+        + [[[dma((n,)), dma((n,))] for n in counts] for _ in range(2)]
+        + [[dma((zr,)), dma((zr,))]],
         compiler_params=pltpu.CompilerParams(
             collective_id=0, has_side_effects=True, vmem_limit_bytes=56 * 1024 * 1024
         ),

time: 209 us -> 169 us (0.81)
  Pallas kernels: 208 us -> 168 us
    pallas_call x1, Pallas kernels: 204 us -> 164 us  [shards(): pl.pallas_call(functools.partial(kernel, xr, zr, dpn, nb, float(tok * seq...]
where the time goes in v3:
time: 169 us
  Pallas kernels  168 us (99%)
    pallas_call x1, Pallas kernels, shards(): pl.pallas_call(functools.partial(kernel, xr, zr, dpn, nb, float(tok * seq...  164 us
    pallas_call x1, Pallas kernels, shards(): pl.pallas_call(functools.partial(hand_over, nb), out_shape=(wide, wide, s...  3.54 us

profile of v3, /device:TPU:1, one launch (start us, length us, event | category | flops | bytes accessed | tf_op | source)
XLA Modules:
  0.0 168.7 jit_solution(6249918236049688006)
XLA Ops:
  0.6 164.5 %mixer.1 = (bf16[128,4096]{1,0:T(8,128)(2,1)}, bf16[128,4096]{1,0:T(8,128)(2,1)}, bf16[128,128]{1,0:T(8,128)(2,1)}, bf16[128,128]{1,0:T(8,128)(2,1)}, f32[40,128]{1,0:T(8,128)}, /*index=5*/f32[8,128]{1,0:T(8,128)}) custom-call(f32[64]{0:T(128)} %lr.1, f32[64]{0:T(128)} %sk.1, bf16[128,4096]{1,0:T(8,128)(2,1)} %bitcast.14, bf16[128,4096]{1,0:T(8,128)(2,1)} %bitcast.15, ...), custom_call_target="tpu_custom_call" | custom-call | tf_op jit(solution)/shard_map/mixer/pallas_call | solution.py:629
  165.1 3.5 %hand_over.1 = (bf16[128,4096]{1,0:T(8,128)(2,1)}, bf16[128,4096]{1,0:T(8,128)(2,1)}, bf16[128,128]{1,0:T(8,128)(2,1)}, bf16[128,128]{1,0:T(8,128)(2,1)}, f32[1,...) custom-call(bf16[128,4096]{1,0:T(8,128)(2,1)} %get-tuple-element.22.gx, ...), custom_call_target="tpu_custom_call" | custom-call | tf_op jit(solution)/shard_map/hand_over/pallas_call | solution.py:667

commit v4 on v3

--- a/solution.py
+++ b/solution.py
@@ -11,7 +11,8 @@
 LANES = 128
 Z_RING = 8
 SPLIT = 2
-HOP = (21, 8)
+HOP = (26, 8)
+PIECES = 4
 
 
 def red8(v):
@@ -33,8 +34,8 @@
 def kernel(
     xr, zr, dpn, nb, rows_total,
     lr, sk, x_in, z_in, tg_in, bk, ck, codes, segs, gains,
-    gx, gz, gb, gc, red, red_rates,
-    x, z, tg,
+    gx_out, gz_out, gb, gc, red, red_rates,
+    x, z, tg, gx, gz,
     f_out, p_st, f_carry, f_part, b_out, r_st, b_carry, b_part,
     mix, ebuf, dxa, inter, ub,
     cols, tab, acc, ga, sa, ra, bt, ct, meta, row_meta,
@@ -209,173 +210,168 @@
             part_down = lambda: self.copy(partial, partial, b, q, sem + 2, 2, self.down).start()
             return wait_recv, wait_carry, wait_part, send_up, carry_down, part_down
 
+        def pieces(self, s, b, body):
+            for q in range(SPLIT):
+                body((b, pl.ds(q * part, part)), *self.moves(s, b, q))
+
+        def scan_up(self, s, b):
+            g = self.own(b)
+
+            def body(cut, wait_recv, _, __, send_up, *___):
+                wait_recv()
+                self.out[cut] = self.out[cut] + g * self.recv[cut]
+                send_up()
+
+            self.pieces(s, b, body)
+
+        def begin_up(self, s, b):
+            self.pieces(s, b, lambda cut, _, __, ___, send_up, *____: send_up())
+            self.recv[b] = jnp.zeros((tok, LANES), F32)
+
+        def reduce_down(self, s, b, send):
+            above = self.decay(1, b)
+
+            def body(cut, _, __, wait_part, ___, ____, part_down):
+                wait_part()
+                self.part[cut] = self.part[cut] + above * self.out[cut]
+                if send:
+                    part_down()
+
+            self.pieces(s, b, body)
+
+        def begin_down(self, s, b):
+            self.part[b] = self.out[b]
+            self.pieces(s, b, lambda cut, _, __, ___, ____, _____, part_down: part_down())
+
+        def spread(self, s, b, send):
+            below = self.decay(0, b)
+
+            def body(cut, _, wait_carry, __, ___, carry_down, ____):
+                wait_carry()
+                if send:
+                    carry_down()
+                self.recv[cut] = self.recv[cut] + below * self.carry[cut]
+
+            self.pieces(s, b, body)
+
+        def arrive(self, s, b):
+            self.pieces(s, b, lambda cut, wait_recv, *_: wait_recv())
+
         def middle_first(self, b):
             p, r = self.p, self.r
-            g, above = self.own(b), self.decay(1, b)
-            for q in range(SPLIT):
-                cut = (b, pl.ds(q * part, part))
-                wait_recv, _, wait_part, send_up, _, part_down = self.moves(0, b, q)
-
-                @pl.when(p < mid)
-                def _():
-                    @pl.when(p > 0)
-                    def _():
-                        wait_recv()
-                        self.out[cut] = self.out[cut] + g * self.recv[cut]
-
-                    @pl.when(p == 0)
-                    def _():
-                        self.recv[cut] = jnp.zeros((part, LANES), F32)
-
-                    send_up()
-
-                @pl.when((p > mid) & (r < xr - 1))
-                def _():
-                    @pl.when(p < zr - 1)
-                    def _():
-                        wait_part()
-                        self.part[cut] = self.part[cut] + above * self.out[cut]
-
-                    @pl.when(p == zr - 1)
-                    def _():
-                        self.part[cut] = self.out[cut]
-
-                    part_down()
+            some = r < xr - 1
+            for when, act in (
+                ((p > 0) & (p < mid), lambda: self.scan_up(0, b)),
+                (p == 0, lambda: self.begin_up(0, b)),
+                ((p > mid) & (p < zr - 1) & some, lambda: self.reduce_down(0, b, True)),
+                ((p == zr - 1) & some, lambda: self.begin_down(0, b)),
+            ):
+                pl.when(when)(act)
 
         def ends_first(self, b):
             p, r = self.p, self.r
-            g, above = self.own(b), self.decay(1, b)
-            for q in range(SPLIT):
-                cut = (b, pl.ds(q * part, part))
-                wait_recv, _, wait_part, send_up, _, part_down = self.moves(1, b, q)
-                to_end = lambda: self.copy(self.out, self.carry, b, q, 6 * self.backward + 3, 1, self.up).start()
-
-                @pl.when(p < mid)
-                def _():
-                    @pl.when(p < mid - 1)
-                    def _():
-                        wait_part()
-                        self.part[cut] = self.part[cut] + above * self.out[cut]
-
-                    @pl.when(p == mid - 1)
-                    def _():
-                        self.part[cut] = self.out[cut]
-
-                    @pl.when(p > 0)
-                    def _():
-                        part_down()
-
-                @pl.when(p >= mid)
-                def _():
-                    @pl.when(p > mid)
-                    def _():
-                        wait_recv()
-                        self.out[cut] = self.out[cut] + g * self.recv[cut]
-
-                    @pl.when(p == mid)
-                    def _():
-                        self.recv[cut] = jnp.zeros((part, LANES), F32)
-
-                    @pl.when(p < zr - 1)
-                    def _():
-                        send_up()
-
-                    @pl.when((p == zr - 1) & (r < xr - 1))
-                    def _():
-                        to_end()
+
+            def at_end():
+                g = self.own(b)
+                for q in range(SPLIT):
+                    cut = (b, pl.ds(q * part, part))
+                    self.moves(1, b, q)[0]()
+                    self.out[cut] = self.out[cut] + g * self.recv[cut]
+
+                    @pl.when(r < xr - 1)
+                    def _():
+                        self.copy(self.out, self.carry, b, q, 6 * self.backward + 3, 1, self.up).start()
+
+            for when, act in (
+                ((p > 0) & (p < mid - 1), lambda: self.reduce_down(1, b, True)),
+                (p == 0, lambda: self.reduce_down(1, b, False)),
+                (p == mid - 1, lambda: self.begin_down(1, b)),
+                (p == mid, lambda: self.begin_up(1, b)),
+                ((p > mid) & (p < zr - 1), lambda: self.scan_up(1, b)),
+                (p == zr - 1, at_end),
+            ):
+                pl.when(when)(act)
 
         def middle_second(self, b):
             p, r = self.p, self.r
-            g = self.own(b)
-            for q in range(SPLIT):
-                cut = (b, pl.ds(q * part, part))
-                wait_recv, wait_carry, wait_part, send_up, carry_down, _ = self.moves(0, b, q)
-                onward = lambda: self.copy(self.part, self.carry, b, q, 6 * self.backward + 2, 1, self.across).start()
-
-                @pl.when((p <= mid) & (r > 0))
-                def _():
-                    wait_carry()
-
-                    @pl.when(p > 0)
-                    def _():
+
+            def root():
+                g, above, low, high, row = self.own(b), *(self.decay(n, b) for n in (1, 2, 3, 4))
+                for q in range(SPLIT):
+                    cut = (b, pl.ds(q * part, part))
+                    wait_recv, wait_carry, wait_part, send_up, carry_down, _ = self.moves(0, b, q)
+                    wait_recv()
+
+                    @pl.when(r < xr - 1)
+                    def _():
+                        wait_part()
+                        self.part[cut] = self.part[cut] + above * self.out[cut] + high * self.recv[cut]
+
+                    @pl.when(r > 0)
+                    def _():
+                        wait_carry()
                         carry_down()
 
-                @pl.when((p < mid) & (r > 0))
-                def _():
-                    self.recv[cut] = self.recv[cut] + self.decay(0, b) * self.carry[cut]
-
-                @pl.when(p >= mid)
-                def _():
-                    wait_recv()
-
-                @pl.when(p == mid)
-                def _():
+                    @pl.when((r > 0) & (r < xr - 1))
+                    def _():
+                        self.part[cut] = self.part[cut] + row * self.carry[cut]
+
                     @pl.when(r < xr - 1)
                     def _():
-                        wait_part()
-                        own = self.part[cut] + self.decay(1, b) * self.out[cut] + self.decay(3, b) * self.recv[cut]
-
-                        @pl.when(r > 0)
-                        def _():
-                            self.part[cut] = own + self.decay(4, b) * self.carry[cut]
-
-                        @pl.when(r == 0)
-                        def _():
-                            self.part[cut] = own
-
-                        onward()
+                        self.copy(self.part, self.carry, b, q, 6 * self.backward + 2, 1, self.across).start()
 
                     @pl.when(r > 0)
                     def _():
-                        self.recv[cut] = self.recv[cut] + self.decay(2, b) * self.carry[cut]
-
-                @pl.when((p >= mid) & (p < zr - 1))
-                def _():
+                        self.recv[cut] = self.recv[cut] + low * self.carry[cut]
+
                     self.out[cut] = self.out[cut] + g * self.recv[cut]
                     send_up()
 
+            for when, act in (
+                ((p > 0) & (p < mid) & (r > 0), lambda: self.spread(0, b, True)),
+                ((p == 0) & (r > 0), lambda: self.spread(0, b, False)),
+                (p == mid, root),
+                ((p > mid) & (p < zr - 1), lambda: self.scan_up(0, b)),
+                (p == zr - 1, lambda: self.arrive(0, b)),
+            ):
+                pl.when(when)(act)
+
         def ends_second(self, b):
             p, r = self.p, self.r
-            g = self.own(b)
-            for q in range(SPLIT):
-                cut = (b, pl.ds(q * part, part))
-                wait_recv, wait_carry, _, send_up, carry_down, _ = self.moves(1, b, q)
-                onward = lambda: self.copy(self.carry, self.recv, b, q, 6 * self.backward + 4, 0, self.across).start()
-                to_end = lambda: self.copy(self.part, self.carry, b, q, 6 * self.backward + 5, 1, self.down).start()
-
-                @pl.when((p < mid) & ((p > 0) | (r > 0)))
-                def _():
-                    wait_recv()
-
-                @pl.when((p == 0) & (r == 0))
-                def _():
-                    self.recv[cut] = jnp.zeros((part, LANES), F32)
-
-                @pl.when((p == 0) & (r < xr - 1))
-                def _():
-                    wait_carry()
-                    self.carry[cut] = self.carry[cut] + self.decay(3, b) * self.part[cut] + self.decay(4, b) * self.recv[cut]
-                    onward()
-
-                @pl.when(p < mid - 1)
-                def _():
+
+            def root():
+                g, low, high, row = self.own(b), *(self.decay(n, b) for n in (2, 3, 4))
+                for q in range(SPLIT):
+                    cut = (b, pl.ds(q * part, part))
+                    wait_recv, wait_carry, _, send_up, *_ = self.moves(1, b, q)
+
+                    @pl.when(r > 0)
+                    def _():
+                        wait_recv()
+
+                    @pl.when(r == 0)
+                    def _():
+                        self.recv[cut] = jnp.zeros((part, LANES), F32)
+
+                    @pl.when(r < xr - 1)
+                    def _():
+                        wait_carry()
+                        self.carry[cut] = self.carry[cut] + high * self.part[cut] + row * self.recv[cut]
+                        self.copy(self.carry, self.recv, b, q, 6 * self.backward + 4, 0, self.across).start()
+
                     self.out[cut] = self.out[cut] + g * self.recv[cut]
                     send_up()
-
-                @pl.when(p == 0)
-                def _():
-                    self.part[cut] = self.part[cut] + self.decay(2, b) * self.recv[cut]
-                    to_end()
-
-                @pl.when(p >= mid)
-                def _():
-                    wait_carry()
-
-                    @pl.when(p > mid)
-                    def _():
-                        carry_down()
-
-                    self.recv[cut] = self.recv[cut] + self.decay(0, b) * self.carry[cut]
+                    self.part[cut] = self.part[cut] + low * self.recv[cut]
+                    self.copy(self.part, self.carry, b, q, 6 * self.backward + 5, 1, self.down).start()
+
+            for when, act in (
+                (p == 0, root),
+                ((p > 0) & (p < mid - 1), lambda: self.scan_up(1, b)),
+                (p == mid - 1, lambda: self.arrive(1, b)),
+                (p == mid, lambda: self.spread(1, b, False)),
+                (p > mid, lambda: self.spread(1, b, True)),
+            ):
+                pl.when(when)(act)
 
         def finish(self):
             p, r = self.p, self.r
@@ -494,11 +490,11 @@
 
     c_mat_ref, b_mat_ref = ck, bk
 
+    pl.semaphore_wait(barrier, len(peers))
+    meta_stage.start(meta[10])
     for load in loads:
         load.wait()
-    pl.semaphore_wait(barrier, len(peers))
-    meta_stage.start(meta[10])
-    fwd.run(block_state, inside, mixture, [(1, take_meta)])
+    fwd.run(block_state, inside, mixture, [(2, take_meta)])
 
     squares = jnp.sum(acc[0], axis=1, keepdims=True)
     r_col = lax.rsqrt(squares * (1.0 / width) + 1e-5)
@@ -569,21 +565,35 @@
     w_stage = [Stage(wide_bufs[i], wide_sems[i], i) for i in range(3)]
     r_stage = [Stage(rate_bufs[i], rate_sems[i], i) for i in range(3)]
 
+    store_gz = pltpu.make_async_copy(gz, gz_out, local.at[3])
+    store_gx = pltpu.make_async_copy(gx, gx_out, local.at[4])
+
     def early_sums():
+        store_gz.start()
         lost = 0.5 * jnp.sum(acc[3, 0:8], axis=1, keepdims=True)
         tile = by_head(sa[...].sum(axis=1)) + jnp.where(lane8 == LANES - 1, lost, 0.0)
         w_stage[0].start(jnp.concatenate([ga[...].sum(axis=1), tile], axis=0))
 
-    bwd.run(direct, inside_back, state_back, [(half - 1 + jnp.maximum(bwd.first[0], bwd.first[1]), early_sums)])
+    def wide_across():
+        w_stage[1].start(w_stage[0].result())
+
+    end = half + jnp.maximum(bwd.second[0], bwd.second[1])
+    made = half - 1 + jnp.maximum(bwd.first[0], bwd.first[1])
+    bwd.run(direct, inside_back, state_back, [(made, early_sums), (jnp.where(bwd.r > 0, end - 4, end), wide_across)])
+    store_gx.start()
 
     a_rows = jnp.concatenate([rates(b)[2] for b in range(nb)], axis=0)
     r_stage[0].start(by_head(ra[...].sum(axis=1) * -a_rows))
-    w_stage[1].start(w_stage[0].result())
+
+    @pl.when(bwd.r == 0)
+    def _():
+        wide_across()
+
+    w_stage[2].start(w_stage[1].result())
     dcb = (acc[5] * tab[3]).astype(BF16)
     gc[...] = (acc[4] + mm(dcb, bk[...])).astype(BF16)
     gb[...] = (acc[6] + mm_tn(dcb, ck[...])).astype(BF16)
     r_stage[1].start(r_stage[0].result())
-    w_stage[2].start(w_stage[1].result())
     r_stage[2].start(r_stage[1].result())
     red[...] = w_stage[2].result() * (1.0 / rows_total)
     fwd.finish()
@@ -591,14 +601,24 @@
     meta_stage.close()
     for stage in w_stage + r_stage[:2]:
         stage.close()
+    store_gz.wait()
+    store_gx.wait()
     red_rates[...] = r_stage[2].result() * (1.0 / rows_total)
     r_stage[2].close()
 
 
-def hand_over(nb, gx, gz, gb, gc, red, red_rates, gx_out, gz_out, gb_out, gc_out, loss, rate, skip, gain, sems):
-    moves = [pltpu.make_async_copy(a, b, sems.at[i]) for i, (a, b) in enumerate(((gx, gx_out), (gz, gz_out)))]
-    for move in moves:
-        move.start()
+def hand_over(nb, gx, gz, gb, gc, red, red_rates, gx_out, gz_out, gb_out, gc_out, loss, rate, skip, gain, stage, sems):
+    rows = gx.shape[0] // PIECES
+    moves = []
+    for i, (src, dst) in enumerate(((gx, gx_out), (gz, gz_out))):
+        for j in range(PIECES):
+            cut, n = pl.ds(j * rows, rows), i * PIECES + j
+            moves.append((
+                pltpu.make_async_copy(src.at[cut], stage.at[i, cut], sems.at[0, n]),
+                pltpu.make_async_copy(stage.at[i, cut], dst.at[cut], sems.at[1, n]),
+            ))
+    for fetch, _ in moves:
+        fetch.start()
     gb_out[...] = gb[...]
     gc_out[...] = gc[...]
     for b in range(nb):
@@ -607,8 +627,11 @@
     loss[...] = tail[:, LANES - 1 :]
     skip[...] = tail[:, : 2 * nb]
     rate[...] = jnp.sum(red_rates[...], axis=0, keepdims=True)[:, : 2 * nb]
-    for move in moves:
-        move.wait()
+    for fetch, store in moves:
+        fetch.wait()
+        store.start()
+    for _, store in moves:
+        store.wait()
 
 
 def shards(mesh, inputs, gates, keys_b, reads_c, step_codes, seg_starts, targets, log_rates, skips, gains):
@@ -630,8 +653,8 @@
         functools.partial(kernel, xr, zr, dpn, nb, float(tok * seq * dpn)),
         out_shape=(wide, wide, small, small, of((rows, LANES), F32), of((8, LANES), F32)),
         in_specs=[smem] * 2 + [hbm] * 3 + [vmem] * 5,
-        out_specs=(vmem,) * 6,
-        scratch_shapes=[half] * 3
+        out_specs=(hbm,) * 2 + (vmem,) * 4,
+        scratch_shapes=[half] * 5
         + [state] * 8
         + [
             flat,
@@ -652,7 +675,7 @@
             [pltpu.VMEM((n, rows, LANES), F32) for n in counts],
             [pltpu.VMEM((n, 8, LANES), F32) for n in counts],
         ]
-        + [[dma((nb * SPLIT,))] * 6, dma((12,)), dma((3,))]
+        + [[dma((nb * SPLIT,))] * 6, dma((12,)), dma((5,))]
         + [[[dma((n,)), dma((n,))] for n in counts] for _ in range(2)]
         + [[dma((zr,)), dma((zr,))]],
         compiler_params=pltpu.CompilerParams(
@@ -667,9 +690,9 @@
     gx, gz, gb, gc, loss, rate, skip, gain = pl.pallas_call(
         functools.partial(hand_over, nb),
         out_shape=(wide, wide, small, small, of((1, 1), F32), line, line, of((1, width), F32)),
-        in_specs=[vmem] * 6,
+        in_specs=[hbm] * 2 + [vmem] * 4,
         out_specs=(hbm,) * 2 + (vmem,) * 6,
-        scratch_shapes=[dma((2,))],
+        scratch_shapes=[pltpu.VMEM((2, tok, width), BF16), dma((2, 2 * PIECES))],
         name="hand_over",
     )(*results)
     return (

time: 169 us -> 159 us (0.941)
  Pallas kernels: 168 us -> 158 us
    pallas_call x1, Pallas kernels: 164 us -> 154 us  [shards(): pl.pallas_call(functools.partial(kernel, xr, zr, dpn, nb, float(tok * seq...]
where the time goes in v4:
time: 159 us
  Pallas kernels  158 us (99%)
    pallas_call x1, Pallas kernels, shards(): pl.pallas_call(functools.partial(kernel, xr, zr, dpn, nb, float(tok * seq...  154 us
    pallas_call x1, Pallas kernels, shards(): pl.pallas_call(functools.partial(hand_over, nb), out_shape=(wide, wide, s...  3.83 us

profile of v4, /device:TPU:1, one launch (start us, length us, event | category | flops | bytes accessed | tf_op | source)
XLA Modules:
  0.0 158.7 jit_solution(9905707310624302743)
XLA Ops:
  0.6 154.3 %mixer.1 = (bf16[128,4096]{1,0:T(8,128)(2,1)}, bf16[128,4096]{1,0:T(8,128)(2,1)}, bf16[128,128]{1,0:T(8,128)(2,1)}, bf16[128,128]{1,0:T(8,128)(2,1)}, f32[40,128]{1,0:T(8,128)}, /*index=5*/f32[8,128]{1,0:T(8,128)}) custom-call(f32[64]{0:T(128)} %lr.1, f32[64]{0:T(128)} %sk.1, bf16[128,4096]{1,0:T(8,128)(2,1)} %bitcast.14, bf16[128,4096]{1,0:T(8,128)(2,1)} %bitcast.15, ...), custom_call_target="tpu_custom_call" | custom-call | tf_op jit(solution)/shard_map/mixer/pallas_call | solution.py:652
  154.9 3.8 %hand_over.1 = (bf16[128,4096]{1,0:T(8,128)(2,1)}, bf16[128,4096]{1,0:T(8,128)(2,1)}, bf16[128,128]{1,0:T(8,128)(2,1)}, bf16[128,128]{1,0:T(8,128)(2,1)}, f32[1,...) custom-call(bf16[128,4096]{1,0:T(8,128)(2,1)} %get-tuple-element.22.gx, ...), custom_call_target="tpu_custom_call" | custom-call | tf_op jit(solution)/shard_map/hand_over/pallas_call | solution.py:690

commit v5 on v4

--- a/solution.py
+++ b/solution.py
@@ -547,7 +547,8 @@
         duw = mm(b_mat_ref[...], byb) * (jnp.exp(-a * cols[1]) * cols[2])
         gx[:, at] = (dxa[:, at] + duw).astype(BF16)
         own = meta[10]
-        ra[b] += red8(cols[1] * duw * x[:, at].astype(F32)) + red8(by * p_st[b]) * (own[0:1] * decay_of(own, a))
+        late = red8(cols[1] * duw * x[:, at].astype(F32)) + red8(by * p_st[b]) * (own[0:1] * decay_of(own, a))
+        ra[b] = (ra[b] + late) * -a
         acc[6] += mm_nt(ub[:, at], byb)
 
     lane8 = lax.broadcasted_iota(jnp.int32, (8, LANES), 1)
@@ -582,8 +583,7 @@
     bwd.run(direct, inside_back, state_back, [(made, early_sums), (jnp.where(bwd.r > 0, end - 4, end), wide_across)])
     store_gx.start()
 
-    a_rows = jnp.concatenate([rates(b)[2] for b in range(nb)], axis=0)
-    r_stage[0].start(by_head(ra[...].sum(axis=1) * -a_rows))
+    r_stage[0].start(by_head(ra[...].sum(axis=1)))
 
     @pl.when(bwd.r == 0)
     def _():

time: 159 us -> 159 us (level)
  no operation moved by 1% of the time
where the time goes in v5:
time: 159 us
  Pallas kernels  158 us (99%)
    pallas_call x1, Pallas kernels, shards(): pl.pallas_call(functools.partial(kernel, xr, zr, dpn, nb, float(tok * seq...  154 us
    pallas_call x1, Pallas kernels, shards(): pl.pallas_call(functools.partial(hand_over, nb), out_shape=(wide, wide, s...  3.83 us

profile of v5, /device:TPU:1, one launch (start us, length us, event | category | flops | bytes accessed | tf_op | source)
XLA Modules:
  0.0 158.7 jit_solution(9702568435075033075)
XLA Ops:
  0.6 154.2 %mixer.1 = (bf16[128,4096]{1,0:T(8,128)(2,1)}, bf16[128,4096]{1,0:T(8,128)(2,1)}, bf16[128,128]{1,0:T(8,128)(2,1)}, bf16[128,128]{1,0:T(8,128)(2,1)}, f32[40,128]{1,0:T(8,128)}, /*index=5*/f32[8,128]{1,0:T(8,128)}) custom-call(f32[64]{0:T(128)} %lr.1, f32[64]{0:T(128)} %sk.1, bf16[128,4096]{1,0:T(8,128)(2,1)} %bitcast.14, bf16[128,4096]{1,0:T(8,128)(2,1)} %bitcast.15, ...), custom_call_target="tpu_custom_call" | custom-call | tf_op jit(solution)/shard_map/mixer/pallas_call | solution.py:652
  154.9 3.8 %hand_over.1 = (bf16[128,4096]{1,0:T(8,128)(2,1)}, bf16[128,4096]{1,0:T(8,128)(2,1)}, bf16[128,128]{1,0:T(8,128)(2,1)}, bf16[128,128]{1,0:T(8,128)(2,1)}, f32[1,...) custom-call(bf16[128,4096]{1,0:T(8,128)(2,1)} %get-tuple-element.22.gx, ...), custom_call_target="tpu_custom_call" | custom-call | tf_op jit(solution)/shard_map/hand_over/pallas_call | solution.py:690
